TPU v7x, 32 devices: a whole 2x2x4 slice. The times are simulated.
32 devices in a mesh: expert: 8 (over z, x), mp: 4 (over y, core).
Axes of the slice: x: 2, y: 2, z: 4, core: 2. Of those that a mesh axis runs over, the one named last changes fastest.
Arguments:
- features: bfloat16 [9456, 768], P('expert'), may hold values from -6 to 6
- norm_gains: float32 [2, 768], P(None, ('expert', 'mp')), may hold values from 0.25 to 1.75
- norm_shifts: float32 [2, 768], P(None, ('expert', 'mp')), may hold values from -0.6 to 0.6
- attention_bias: float32 [2, 768], P(None, ('expert', 'mp')), may hold values from -0.6 to 0.6
- output_bias: float32 [768], P(('expert', 'mp')), may hold values from -0.6 to 0.6
- project_weight: float32 [768, 3, 768], P('expert', None, 'mp'), may hold values from -0.21875 to 0.21875
- merge_weight: float32 [768, 768], P('mp', 'expert'), may hold values from -0.625 to 0.625
- router_weight: float32 [768, 8], P('expert'), may hold values from -0.15625 to 0.15625
- router_noise: float32 [9456, 8], P('expert'), may hold values from -1.8 to 1.8
- routes: int32 [9456, 2], P('expert'), may hold values from 0 to 7, as said below
- slot_numbers: int32 [9456, 2], P('expert'), may hold values from 0 to 442, as said below
- expand_weight: float32 [8, 768, 3072], P('expert', None, 'mp'), may hold values from -0.21875 to 0.21875
- expand_bias: float32 [8, 3072], P('expert', 'mp'), may hold values from -0.6 to 0.6
- contract_weight: float32 [8, 3072, 768], P('expert', 'mp'), may hold values from -0.15625 to 0.15625
- contract_bias: float32 [8, 768], P('expert'), may hold values from -0.6 to 0.6
- cotangent: float32 [9456, 768], P('expert'), may hold values from -6 to 6
Outputs:
- block_output: bfloat16 [9456, 768], P('expert', 'mp')
- feature_grad: float32 [9456, 768], P('expert')
- gain_grad: float32 [2, 768], P(None, ('expert', 'mp'))
- shift_grad: float32 [2, 768], P(None, ('expert', 'mp'))
- attention_bias_grad: float32 [2, 768], P(None, ('expert', 'mp'))
- output_bias_grad: float32 [768], P(('expert', 'mp'))
- project_grad: float32 [768, 3, 768], P('expert', None, 'mp')
- merge_grad: float32 [768, 768], P('mp', 'expert')
- router_grad: float32 [768, 8], P('expert')
- expand_grad: float32 [8, 768, 3072], P('expert', None, 'mp')
- expand_bias_grad: float32 [8, 3072], P('expert', 'mp')
- contract_grad: float32 [8, 3072, 768], P('expert', 'mp')
- contract_bias_grad: float32 [8, 768], P('expert')
Inputs may be any that keep to these rules, and one draw needn't show every extreme that they name: `routes`: in each aligned block of 1182 rows (the tokens of one index of the expert axis) the two entries of a row differ, every expert is named at least once and at most 443 times, and some expert is named exactly 443 times. `slot_numbers`: in each aligned block of 1182 rows, the routes that name one expert carry distinct slot numbers 0 to their count minus one.
All inputs are finite; a program needn't handle non-finite values.
Results may differ from a plain program's by a relative error of at most 0.02.
Values may be sent and summed in bfloat16 or wider, within the bound.
A program may use at most 192 MiB of HBM per device.

v0:
```python
import jax
import jax.numpy as jnp
from jax import lax
from jax.sharding import PartitionSpec as P

HEAD = 64
SEQ = 197


eps_norm = 1e-06


def norm_parts(value):
    mean_value = jnp.mean(value, axis=-1, keepdims=True)
    centred = value - mean_value
    variance = jnp.mean(centred * centred, axis=-1, keepdims=True)
    inverse = lax.rsqrt(variance + eps_norm)
    return (centred * inverse, inverse)


def norm_back(grad_normed, normed, inverse):
    mean_grad = jnp.mean(grad_normed, axis=-1, keepdims=True)
    mean_mixed = jnp.mean(grad_normed * normed, axis=-1, keepdims=True)
    return inverse * (grad_normed - mean_grad - normed * mean_mixed)


def dot_transposed(first_matrix, second_matrix):
    return lax.dot_general(
        first_matrix, second_matrix, (((1,), (1,)), ((), ())), preferred_element_type=jnp.float32
    )


def transposed_dot(first_matrix, second_matrix):
    return lax.dot_general(
        first_matrix, second_matrix, (((0,), (0,)), ((), ())), preferred_element_type=jnp.float32
    )


def exact_gelu(value):
    return jax.nn.gelu(value, approximate=False)


def heads_total(partial_value):
    return lax.psum(partial_value.astype(jnp.bfloat16), "mp").astype(jnp.float32)


def to_owner(buffer):
    arrived = lax.all_to_all(buffer, "expert", split_axis=0, concat_axis=0, tiled=True)
    return arrived.reshape(-1, arrived.shape[2])


def to_source(partial_value, shift_row, capacity):
    summed = lax.psum(partial_value.astype(jnp.bfloat16), "mp").astype(jnp.float32) + shift_row
    rounded = summed.astype(jnp.bfloat16).reshape(-1, capacity, summed.shape[1])
    returned = lax.all_to_all(rounded, "expert", split_axis=0, concat_axis=0, tiled=True)
    return returned.reshape(-1, returned.shape[2])


def on_device(
    features,
    norm_gains,
    norm_shifts,
    attention_bias,
    output_bias,
    project_weight,
    merge_weight,
    router_weight,
    router_noise,
    routes,
    slot_numbers,
    expand_weight,
    expand_bias,
    contract_weight,
    contract_bias,
    cotangent,
):
    token_count, model_width = features.shape
    narrow_count = lax.axis_size("mp")
    narrow_index = lax.axis_index("mp")
    owners = lax.axis_size("expert")
    capacity = 3 * token_count // owners
    quarter_width = model_width // narrow_count
    local_heads = quarter_width // HEAD
    images = token_count // SEQ
    route_count = routes.shape[1]
    score_scale = HEAD ** (-0.5)
    project_low, merge_low, router_low = (
        lax.all_gather(project_weight.astype(jnp.bfloat16), "expert", axis=0, tiled=True),
        lax.all_gather(merge_weight.astype(jnp.bfloat16), "expert", axis=1, tiled=True),
        lax.all_gather(router_weight.astype(jnp.bfloat16), "expert", axis=0, tiled=True),
    )
    gains, shifts, bias_full, out_shift = (
        lax.all_gather(norm_gains, ("expert", "mp"), axis=1, tiled=True),
        lax.all_gather(norm_shifts, ("expert", "mp"), axis=1, tiled=True),
        lax.all_gather(attention_bias, ("expert", "mp"), axis=1, tiled=True),
        lax.all_gather(output_bias, ("expert", "mp"), axis=0, tiled=True),
    )
    bias_local = lax.dynamic_slice_in_dim(bias_full, narrow_index * quarter_width, quarter_width, 1)
    input_rows = features.astype(jnp.float32)
    first_normed, first_inverse = norm_parts(input_rows)
    normed = (first_normed * gains[0] + shifts[0]).astype(jnp.bfloat16)
    projections = jnp.einsum("td,dcf->ctf", normed, project_low, preferred_element_type=jnp.float32)
    head_shape = (images, SEQ, local_heads, HEAD)
    query = (projections[0] + bias_local[0]).astype(jnp.bfloat16).reshape(head_shape)
    key_rows = projections[1].astype(jnp.bfloat16).reshape(head_shape)
    values = (projections[2] + bias_local[1]).astype(jnp.bfloat16).reshape(head_shape)
    scores = (
        jnp.einsum("bqhe,bkhe->bhqk", query, key_rows, preferred_element_type=jnp.float32)
        * score_scale
    )
    row_peak = jnp.max(scores, axis=-1, keepdims=True)
    exponent = jnp.exp(scores - row_peak)
    row_total = jnp.sum(exponent, axis=-1, keepdims=True)
    attn_weights = exponent / row_total
    log_total = row_peak + jnp.log(row_total)
    attended = jnp.einsum(
        "bhqk,bkhe->bqhe",
        attn_weights.astype(jnp.bfloat16),
        values,
        preferred_element_type=jnp.float32,
    )
    attended = attended.reshape(token_count, quarter_width).astype(jnp.bfloat16)
    projected = heads_total(jnp.dot(attended, merge_low, preferred_element_type=jnp.float32))
    hidden = input_rows + projected + out_shift
    second_normed, second_inverse = norm_parts(hidden)
    routed = (second_normed * gains[1] + shifts[1]).astype(jnp.bfloat16)
    expert_total = router_low.shape[1]
    chosen = (
        routes[:, :, None] == jnp.arange(expert_total, dtype=jnp.int32)[None, None, :]
    ).astype(jnp.float32)
    logits = jnp.dot(routed, router_low, preferred_element_type=jnp.float32) + router_noise
    picked = jnp.einsum("tke,te->tk", chosen, logits, precision=lax.Precision.HIGHEST)
    gate_values = jax.nn.softmax(picked, axis=1)
    slot_index = (routes * capacity + slot_numbers).reshape(-1)
    buffer = (
        jnp.zeros((owners * capacity, model_width), jnp.bfloat16)
        .at[slot_index]
        .set(jnp.repeat(routed, route_count, axis=0))
    )
    arrived = to_owner(buffer.reshape(owners, capacity, model_width))
    expand_low = expand_weight[0].astype(jnp.bfloat16)
    contract_low = contract_weight[0].astype(jnp.bfloat16)
    inner_value = jnp.dot(arrived, expand_low, preferred_element_type=jnp.float32) + expand_bias[0]
    active, gelu_back = jax.vjp(exact_gelu, inner_value)
    active_low = active.astype(jnp.bfloat16)
    expert_partial = jnp.dot(active_low, contract_low, preferred_element_type=jnp.float32)
    returned = to_source(expert_partial, contract_bias[0], capacity)
    picked_rows = (
        returned[slot_index].reshape(token_count, route_count, model_width).astype(jnp.float32)
    )
    combined = jnp.sum(gate_values[:, :, None] * picked_rows, axis=1)
    output = hidden + combined
    block_output = lax.dynamic_slice_in_dim(
        output, narrow_index * quarter_width, quarter_width, 1
    ).astype(jnp.bfloat16)
    gate_grad = jnp.sum(picked_rows * cotangent[:, None, :], axis=2)
    select_grad = gate_values * (
        gate_grad - jnp.sum(gate_values * gate_grad, axis=1, keepdims=True)
    )
    logit_grad = jnp.einsum(
        "tke,tk->te", chosen, select_grad, precision=lax.Precision.HIGHEST
    ).astype(jnp.bfloat16)
    row_grad = (
        (gate_values[:, :, None] * cotangent[:, None, :])
        .astype(jnp.bfloat16)
        .reshape(-1, model_width)
    )
    grad_buffer = (
        jnp.zeros((owners * capacity, model_width), jnp.bfloat16).at[slot_index].set(row_grad)
    )
    grad_arrived = to_owner(grad_buffer.reshape(owners, capacity, model_width))
    active_grad = dot_transposed(grad_arrived, contract_low)
    inner_grad = gelu_back(active_grad)[0].astype(jnp.bfloat16)
    contract_grad = transposed_dot(active_low, grad_arrived)
    contract_bias_grad = jnp.sum(grad_arrived.astype(jnp.float32), axis=0)
    expand_grad = transposed_dot(arrived, inner_grad)
    expand_bias_grad = jnp.sum(inner_grad.astype(jnp.float32), axis=0)
    arrived_grad = dot_transposed(inner_grad, expand_low)
    sent_grad = to_source(arrived_grad, jnp.zeros((model_width,), jnp.float32), capacity)
    routed_grad = jnp.sum(
        sent_grad[slot_index].reshape(token_count, route_count, model_width).astype(jnp.float32),
        axis=1,
    )
    routed_grad = routed_grad + dot_transposed(logit_grad, router_low)
    router_grad = transposed_dot(routed, logit_grad)
    second_gain_grad = jnp.sum(routed_grad * second_normed, axis=0)
    second_shift_grad = jnp.sum(routed_grad, axis=0)
    hidden_grad = cotangent + norm_back(routed_grad * gains[1], second_normed, second_inverse)
    out_shift_grad = jnp.sum(hidden_grad, axis=0)
    projected_grad = hidden_grad.astype(jnp.bfloat16)
    merge_grad = transposed_dot(attended, projected_grad)
    attended_grad = (
        dot_transposed(projected_grad, merge_low).astype(jnp.bfloat16).reshape(head_shape)
    )
    again = (
        jnp.einsum("bqhe,bkhe->bhqk", query, key_rows, preferred_element_type=jnp.float32)
        * score_scale
    )
    again_weights = jnp.exp(again - log_total)
    weight_grad = jnp.einsum(
        "bqhe,bkhe->bhqk", attended_grad, values, preferred_element_type=jnp.float32
    )
    values_grad = jnp.einsum(
        "bhqk,bqhe->bkhe",
        again_weights.astype(jnp.bfloat16),
        attended_grad,
        preferred_element_type=jnp.float32,
    )
    score_grad = (
        again_weights * (weight_grad - jnp.sum(again_weights * weight_grad, axis=-1, keepdims=True))
    ).astype(jnp.bfloat16)
    query_grad = (
        jnp.einsum("bhqk,bkhe->bqhe", score_grad, key_rows, preferred_element_type=jnp.float32)
        * score_scale
    )
    key_grad = (
        jnp.einsum("bhqk,bqhe->bkhe", score_grad, query, preferred_element_type=jnp.float32)
        * score_scale
    )
    stacked_grad = (
        jnp.stack([query_grad, key_grad, values_grad])
        .reshape(3, token_count, quarter_width)
        .astype(jnp.bfloat16)
    )
    project_grad = jnp.einsum(
        "td,ctf->dcf", normed, stacked_grad, preferred_element_type=jnp.float32
    )
    local_bias_grad = jnp.stack(
        [
            jnp.sum(stacked_grad[0].astype(jnp.float32), axis=0),
            jnp.sum(stacked_grad[2].astype(jnp.float32), axis=0),
        ]
    )
    normed_grad = heads_total(
        jnp.einsum("ctf,dcf->td", stacked_grad, project_low, preferred_element_type=jnp.float32)
    )
    first_gain_grad = jnp.sum(normed_grad * first_normed, axis=0)
    first_shift_grad = jnp.sum(normed_grad, axis=0)
    feature_grad = hidden_grad + norm_back(normed_grad * gains[0], first_normed, first_inverse)
    own_columns = (
        jnp.arange(model_width, dtype=jnp.int32) // quarter_width == narrow_index
    ).astype(jnp.float32)
    gain_terms = jnp.stack([first_gain_grad, second_gain_grad]) * own_columns
    shift_terms = jnp.stack([first_shift_grad, second_shift_grad]) * own_columns
    bias_terms = lax.dynamic_update_slice_in_dim(
        jnp.zeros((2, model_width), jnp.float32), local_bias_grad, narrow_index * quarter_width, 1
    )
    out_terms = out_shift_grad * own_columns
    gain_grad, shift_grad, attention_bias_grad, output_bias_grad = (
        lax.psum_scatter(gain_terms, ("expert", "mp"), scatter_dimension=1, tiled=True),
        lax.psum_scatter(shift_terms, ("expert", "mp"), scatter_dimension=1, tiled=True),
        lax.psum_scatter(bias_terms, ("expert", "mp"), scatter_dimension=1, tiled=True),
        lax.psum_scatter(out_terms, ("expert", "mp"), scatter_dimension=0, tiled=True),
    )
    project_share, merge_share, router_share = (
        lax.psum_scatter(project_grad, "expert", scatter_dimension=0, tiled=True),
        lax.psum_scatter(merge_grad, "expert", scatter_dimension=1, tiled=True),
        lax.psum_scatter(router_grad, "expert", scatter_dimension=0, tiled=True),
    )
    return (
        block_output,
        feature_grad,
        gain_grad,
        shift_grad,
        attention_bias_grad,
        output_bias_grad,
        project_share,
        merge_share,
        router_share,
        expand_grad[None],
        expand_bias_grad[None],
        contract_grad[None],
        contract_bias_grad[None],
    )


def solution(mesh):
    placed = (
        P("expert", None),
        P(None, ("expert", "mp")),
        P(None, ("expert", "mp")),
        P(None, ("expert", "mp")),
        P(("expert", "mp")),
        P("expert", None, "mp"),
        P("mp", "expert"),
        P("expert", None),
        P("expert", None),
        P("expert", None),
        P("expert", None),
        P("expert", None, "mp"),
        P("expert", "mp"),
        P("expert", "mp", None),
        P("expert", None),
        P("expert", None),
    )
    return jax.shard_map(
        on_device,
        mesh=mesh,
        in_specs=placed,
        out_specs=(
            P("expert", "mp"),
            P("expert", None),
            P(None, ("expert", "mp")),
            P(None, ("expert", "mp")),
            P(None, ("expert", "mp")),
            P(("expert", "mp")),
            P("expert", None, "mp"),
            P("mp", "expert"),
            P("expert", None),
            P("expert", None, "mp"),
            P("expert", "mp"),
            P("expert", "mp", None),
            P("expert", None),
        ),
        check_vma=False,
    )
```

profile of v0, /device:TPU:0, one launch (start us, length us, event | category | flops | bytes accessed | tf_op | source)
XLA Modules:
  0.0 1462.3 jit_solution(14892709792439223560)
XLA Ops:
  11.5 43.3 %all-gather = f32[32,24,2]{1,2,0:T(2,128)S(1)} all-gather(f32[1,24,2]{1,2,0:T(2,128)S(1)} %bitcast.133), channel_id=1, replica_groups=mesh['expert'=8,'mp'=4] {'expert','mp'}, dimensions={0}, use_global_device_ids=true | all-gather | bytes 6336 | tf_op jit(solution)/shard_map/all_gather | solution.py:93
  54.9 36.7 %all-gather.1 = f32[32,24,2]{1,2,0:T(2,128)S(1)} all-gather(f32[1,24,2]{1,2,0:T(2,128)S(1)} %bitcast.134), channel_id=1, replica_groups=mesh['expert'=8,'mp'=4] {'expert','mp'}, dimensions={0}, use_global_device_ids=true | all-gather | bytes 6336 | tf_op jit(solution)/shard_map/all_gather | solution.py:94
  91.8 37.1 %all_gather.23 = bf16[768,3,192]{2,1,0:T(4,128)(2,1)S(1)} all-gather(bf16[96,3,192]{2,1,0:T(4,128)(2,1)S(1)} %copy.123), channel_id=1, replica_groups=mesh['expert'=8,'mp'=4] {'expert'}, dimensions={0}, use_global_device_ids=true | all-gather | bytes 995328 | tf_op jit(solution)/shard_map/all_gather | solution.py:88
  135.1 39.6 %all-gather.2 = f32[32,24,2]{1,2,0:T(2,128)S(1)} all-gather(f32[1,24,2]{1,2,0:T(2,128)S(1)} %bitcast.135), channel_id=1, replica_groups=mesh['expert'=8,'mp'=4] {'expert','mp'}, dimensions={0}, use_global_device_ids=true | all-gather | bytes 6336 | tf_op jit(solution)/shard_map/all_gather | solution.py:95
  175.2 33.4 %all_gather.25 = bf16[192,768]{0,1:T(8,128)(2,1)} all-gather(bf16[192,96]{0,1:T(8,128)(2,1)S(1)} %copy.131), channel_id=1, replica_groups=mesh['expert'=8,'mp'=4] {'expert'}, dimensions={1}, use_global_device_ids=true | all-gather | bytes 331776 | tf_op jit(solution)/shard_map/all_gather | solution.py:89
  224.5 38.2 %all-reduce = f32[768]{0:T(1024)S(1)} all-reduce(f32[768]{0:T(1024)S(1)} %dynamic-update-slice), channel_id=1, replica_groups=mesh['expert'=8,'mp'=4] {'expert','mp'}, use_global_device_ids=true, to_apply=%add | all-reduce | flops 768 | bytes 6144
  290.0 17.0 %scatter_custom_fusion = bf16[3544,768]{1,0:T(8,128)(2,1)} fusion(s32[2364]{0:T(1024)S(1)} %fusion.79, bf16[2364,768]{1,0:T(8,128)(2,1)} %reshape.247, bf16[]{:T(256)} %constant.17.clone.1), kind=kCustom, calls=%fused_computation.72 | custom fusion | bytes 5444096 | tf_op jit(solution)/shard_map/scatter | solution.py:138
  319.2 139.7 %all-gather.3 = bf16[8,96,8]{1,2,0:T(8,128)(2,1)S(1)} all-gather(bf16[1,96,8]{1,2,0:T(8,128)(2,1)S(1)} %convert_bitcast_fusion), channel_id=1, replica_groups=mesh['expert'=8,'mp'=4] {'expert'}, dimensions={0}, use_global_device_ids=true | all-gather | bytes 13824 | tf_op jit(solution)/shard_map/all_gather | solution.py:90
  479.0 24.6 %scatter_custom_fusion.1 = bf16[3544,768]{1,0:T(8,128)(2,1)} fusion(s32[2364]{0:T(1024)S(1)} %fusion.79, f32[2364,768]{1,0:T(8,128)} %mul.240, f32[2364]{0:T(1024)S(1)} %mul.237, bf16[]{:T(256)} %constant.17.clone.1), kind=kCustom, calls=%fused_computation.58 | custom fusion | flops 3631104 | bytes 12718082 | tf_op jit(solution)/shard_map/scatter | solution.py:169
  521.7 31.2 %multiply_convert_fusion = (bf16[3544,768]{1,0:T(8,128)(2,1)S(1)}, f32[3544,768]{1,0:T(8,128)}, f32[3544,768]{1,0:T(8,128)}) fusion(f32[768]{0:T(1024)S(1)} %reduce.15, bf16[3544,768]{1,0:T(8,128)(2,1)} %reshape.217, f32[1,768,768]{2,1,0:T(8,128)} %param.27), kind=kOutput, calls=%fused_computation.10 | convolution fusion | flops 4360900608 | bytes 35023872 | tf_op jit(solution)/shard_map/dot_general | solution.py:143
  561.5 70.3 %all-to-all-done.2 = bf16[8,443,768]{2,1,0:T(8,128)(2,1)} async-done(((bf16[8,443,768]{2,1,0:T(8,128)(2,1)}), bf16[8,443,768]{2,1,0:T(8,128)(2,1)}, u32[]{:S(2)}, u32[]{:S(2)}) %all-to-all-start.2) | async-done | bytes 5443616 | tf_op jit(solution)/shard_map/all_to_all | solution.py:48
  638.5 13.3 convert_reduce_fusion.1
  667.4 193.5 %all-reduce.15.cloned.1.call-done = (bf16[3544,768]{1,0:T(8,128)(2,1)}, bf16[8,443,768]{2,1,0:T(8,128)(2,1)}) async-done(((bf16[3544,768]{1,0:T(8,128)(2,1)}, bf16[8,443,768]{2,1,0:T(8,128)(2,1)}), (bf16[3544,768]{1,0:T(8,128)(2,1)}, bf16[8,443,768]{2,1,0:T(8,128)(2,1)})) %all-reduce.15.cloned.1.call-update) | async-done | bytes 10887184 | tf_op jit(solution)/shard_map/psum | solution.py:53
  879.1 108.9 %all-to-all-done.3 = bf16[8,443,768]{2,1,0:T(8,128)(2,1)} async-done(((bf16[8,443,768]{2,1,0:T(8,128)(2,1)}), bf16[8,443,768]{2,1,0:T(8,128)(2,1)}, u32[]{:S(2)}, u32[]{:S(2)}) %all-to-all-start.3) | async-done | bytes 5443616 | tf_op jit(solution)/shard_map/all_to_all | solution.py:55
  1000.8 13.5 gather_fusion.1
  1014.3 99.0 %all-to-all-done.1 = bf16[8,443,768]{2,1,0:T(8,128)(2,1)} async-done(((bf16[8,443,768]{2,1,0:T(8,128)(2,1)}), bf16[8,443,768]{2,1,0:T(8,128)(2,1)}, u32[]{:S(2)}, u32[]{:S(2)}) %all-to-all-start.1) | async-done | bytes 5443616 | tf_op jit(solution)/shard_map/all_to_all | solution.py:55
  1119.9 13.5 gather_fusion
  1142.5 19.7 %multiply_reduce_fusion = (f32[1182,2]{1,0:T(8,128)S(1)}, f32[1182,768]{1,0:T(8,128)}) fusion(f32[1182,2,768]{2,1,0:T(2,128)} %reshape.225, f32[1182,768]{1,0:T(8,128)} %param.31, f32[1182,2]{1,0:T(8,128)S(1)} %copy-done.14), kind=kLoop, calls=%fused_computation.25 | loop fusion | flops 6352068 | bytes 14543328 | tf_op jit(solution)/shard_map/reduce_sum | solution.py:156
  1180.5 11.7 reduce_sum.223
  1251.0 18.1 %reduce-scatter.15.cloned.1.call-done = f32[96,8]{1,0:T(8,128)} async-done(((f32[768,8]{1,0:T(8,128)}), f32[96,8]{1,0:T(8,128)}) %reduce-scatter.15.cloned.1.call-update) | async-done | bytes 3088
  1270.5 46.9 %all-reduce.13.cloned.1.call-done = bf16[1182,768]{1,0:T(8,128)(2,1)} async-done(((bf16[1182,768]{1,0:T(8,128)(2,1)}), bf16[1182,768]{1,0:T(8,128)(2,1)}) %all-reduce.13.cloned.1.call-update) | async-done | bytes 1815568 | tf_op jit(solution)/shard_map/psum | solution.py:44
  1320.8 39.9 %all-reduce.5 = (f32[2,768]{1,0:T(2,128)S(1)}, f32[2,768]{1,0:T(2,128)S(1)}, f32[2,768]{1,0:T(2,128)S(1)}, f32[768]{0:T(1024)S(1)}) all-reduce(f32[2,768]{1,0:T(2,128)S(1)} %get-tuple-element.109, f32[2,768]{1,0:T(2,128)S(1)} %get-tuple-element.108, ...), channel_id=2, replica_groups=mesh['expert'=8,'mp'=4] {'expert','mp'}, use_global_device_ids=true, to_apply=%region_25.0.clone | all-reduce | flops 5376 | bytes 43008
  1367.6 15.3 %reduce-scatter.13.cloned.1.call-done = f32[96,192]{1,0:T(8,128)} async-done(((f32[768,192]{1,0:T(8,128)}), f32[96,192]{1,0:T(8,128)}) %reduce-scatter.13.cloned.1.call-update) | async-done | bytes 73744
  1384.6 70.7 %reduce-scatter.11.cloned.1.call-done = f32[96,3,192]{2,0,1:T(8,128)} async-done(((f32[768,3,192]{2,0,1:T(8,128)}), f32[96,3,192]{2,0,1:T(8,128)}) %reduce-scatter.11.cloned.1.call-update) | async-done | bytes 221200 | tf_op jit(solution)/shard_map/reduce_scatter | solution.py:256
  (291 shorter events, 271.9 us)
Async XLA Ops:
  7.2 47.7 %copy-start.63 = (f32[2,24]{1,0:T(2,128)S(1)}, f32[2,24]{1,0:T(2,128)}, u32[]{:S(2)}) copy-start(f32[2,24]{1,0:T(2,128)} %param.18) | copy-start | bytes 580
  7.2 84.4 %copy-start.25 = (f32[96,3,192]{2,0,1:T(8,128)S(1)}, f32[96,3,192]{2,0,1:T(8,128)}, u32[]{:S(2)}) copy-start(f32[96,3,192]{2,0,1:T(8,128)} %param.21) | copy-start | bytes 663556
  7.2 261.0 %all-reduce.11.cloned.1.call-start = ((), (), s32[]{:S(2)}) async-start(), calls=%async_computation.7 | async-start | bytes 3637248 | tf_op jit(solution)/shard_map/psum | solution.py:44
  9.1 121.8 %copy-start.6 = (bf16[1182,768]{1,0:T(8,128)(2,1)S(1)}, bf16[1182,768]{1,0:T(8,128)(2,1)}, u32[]{:S(2)}) copy-start(bf16[1182,768]{1,0:T(8,128)(2,1)} %param.16) | copy-start | bytes 5446660
  9.1 124.5 %copy-start.36 = (f32[1182]{0:T(1024)}, f32[1182]{0:T(1024)S(1)}, u32[]{:S(2)}) copy-start(f32[1182]{0:T(1024)S(1)} %broadcast_multiply_fusion.5) | copy-start | bytes 14188
  11.5 122.2 %copy-start.47 = (f32[1182]{0:T(1024)}, f32[1182]{0:T(1024)S(1)}, u32[]{:S(2)}) copy-start(f32[1182]{0:T(1024)S(1)} %add_rsqrt_fusion.1) | copy-start | bytes 14188
  130.9 140.1 %copy-start.49 = (f32[768]{0:T(1024)}, f32[768]{0:T(1024)S(1)}, u32[]{:S(2)}) copy-start(f32[768]{0:T(1024)S(1)} %get-tuple-element.119) | copy-start | bytes 9220
  133.7 41.4 %copy-start.44 = (f32[192,96]{1,0:T(8,128)S(1)}, f32[192,96]{1,0:T(8,128)}, u32[]{:S(2)}) copy-start(f32[192,96]{1,0:T(8,128)} %param.22) | copy-start | bytes 221188
  221.5 48.9 %copy-start.19 = (bf16[1182,192]{0,1:T(8,128)(2,1)}, bf16[1182,192]{0,1:T(8,128)(2,1)S(1)}, u32[]{:S(2)}) copy-start(bf16[1182,192]{0,1:T(8,128)(2,1)S(1)} %convert_element_type.160) | copy-start | bytes 1361668
  262.7 216.3 %copy-start.51 = (s32[2364]{0:T(1024)}, s32[2364]{0:T(1024)S(1)}, u32[]{:S(2)}) copy-start(s32[2364]{0:T(1024)S(1)} %fusion.79) | copy-start | bytes 28372
  272.7 203.6 %copy-start.9 = (bf16[1182,768]{1,0:T(8,128)(2,1)}, bf16[1182,768]{1,0:T(8,128)(2,1)S(1)}, u32[]{:S(2)}) copy-start(bf16[1182,768]{1,0:T(8,128)(2,1)S(1)} %add_convert_fusion.2) | copy-start | bytes 5446660
  313.6 196.7 %all-to-all-start = ((bf16[8,443,768]{2,1,0:T(8,128)(2,1)}), bf16[8,443,768]{2,1,0:T(8,128)(2,1)}, u32[]{:S(2)}, u32[]{:S(2)}) async-start(bf16[8,443,768]{2,1,0:T(8,128)(2,1)} %reshape.216), calls=%async_computation | async-start | bytes 11010048 | tf_op jit(solution)/shard_map/all_to_all | solution.py:48
  510.3 121.6 %all-to-all-start.2 = ((bf16[8,443,768]{2,1,0:T(8,128)(2,1)}), bf16[8,443,768]{2,1,0:T(8,128)(2,1)}, u32[]{:S(2)}, u32[]{:S(2)}) async-start(bf16[8,443,768]{2,1,0:T(8,128)(2,1)} %reshape.220), calls=%async_computation.2 | async-start | bytes 11010048 | tf_op jit(solution)/shard_map/all_to_all | solution.py:48
  515.1 345.8 %all-reduce.15.cloned.1.call-start = ((), (), s32[]{:S(2)}) async-start(), calls=%async_computation.12 | async-start | bytes 21897216 | tf_op jit(solution)/shard_map/psum | solution.py:53
  860.9 127.2 %all-to-all-start.3 = ((bf16[8,443,768]{2,1,0:T(8,128)(2,1)}), bf16[8,443,768]{2,1,0:T(8,128)(2,1)}, u32[]{:S(2)}, u32[]{:S(2)}) async-start(bf16[8,443,768]{2,1,0:T(8,128)(2,1)} %get-tuple-element.99), calls=%async_computation.3 | async-start | bytes 11010048 | tf_op jit(solution)/shard_map/all_to_all | solution.py:55
  879.1 113.7 %copy-start.46 = (s32[1182,2]{0,1:T(2,128)S(1)}, s32[1182,2]{0,1:T(2,128)}, u32[]{:S(2)}) copy-start(s32[1182,2]{0,1:T(2,128)} %param.25) | copy-start | bytes 28372
  879.1 115.1 %copy-start.52 = (s32[2364]{0:T(1024)S(1)}, s32[2364]{0:T(1024)}, u32[]{:S(2)}) copy-start(s32[2364]{0:T(1024)} %copy-done.51) | copy-start | bytes 28372
  879.1 115.1 %copy-start.27 = (f32[6,3,197]{2,1,0:T(4,128)S(1)}, f32[6,3,197]{2,1,0:T(4,128)}, u32[]{:S(2)}) copy-start(f32[6,3,197]{2,1,0:T(4,128)} %copy-done.26) | copy-start | bytes 42556
  879.1 115.1 %copy-start.43 = (f32[6,3,197]{2,1,0:T(4,128)S(1)}, f32[6,3,197]{2,1,0:T(4,128)}, u32[]{:S(2)}) copy-start(f32[6,3,197]{2,1,0:T(4,128)} %copy-done.42) | copy-start | bytes 42556
  988.1 125.2 %all-to-all-start.1 = ((bf16[8,443,768]{2,1,0:T(8,128)(2,1)}), bf16[8,443,768]{2,1,0:T(8,128)(2,1)}, u32[]{:S(2)}, u32[]{:S(2)}) async-start(bf16[8,443,768]{2,1,0:T(8,128)(2,1)} %reshape.218), calls=%async_computation.1 | async-start | bytes 11010048 | tf_op jit(solution)/shard_map/all_to_all | solution.py:55
  992.7 276.3 %reduce-scatter.15.cloned.1.call-start = ((), (), s32[]{:S(2)}) async-start(), calls=%async_computation.11 | async-start | bytes 442368
  1209.4 107.9 %all-reduce.13.cloned.1.call-start = ((), (), s32[]{:S(2)}) async-start(), calls=%async_computation.8 | async-start | bytes 3637248 | tf_op jit(solution)/shard_map/psum | solution.py:44
  1217.9 165.0 %reduce-scatter.13.cloned.1.call-start = ((), (), s32[]{:S(2)}) async-start(), calls=%async_computation.10 | async-start | bytes 884736
  1229.2 226.0 %reduce-scatter.11.cloned.1.call-start = ((), (), s32[]{:S(2)}) async-start(), calls=%async_computation.9 | async-start | bytes 2654208 | tf_op jit(solution)/shard_map/reduce_scatter | solution.py:256
  (56 other events, 439.9 us)
Sparse Core Ops, SparseCore 0:
  223.6 44.5 all-reduce.10
  667.5 193.3 all-reduce.14
  1209.6 59.4 reduce-scatter.14
  1271.3 46.0 all-reduce.12
  1320.5 62.3 reduce-scatter.12
  1387.3 67.9 reduce-scatter.10
where the time goes:
time: 1470 us; the launch traced here: 1460 us
  waiting for transfers between devices  628 us (43%)
  blocking collectives  408 us (28%)
  local copies, waits for them, and re-layouts  187 us (13%)
  matrix products  111 us (8%)
  other arithmetic  91.9 us (6%)
  starting transfers between devices  21 us (1%)
  between operations  15.5 us (1%)
    all_to_all x2, waiting for transfers between devices, to_source(): lax.all_to_all(rounded, 'expert', split_axis=0, concat_axis=0, tiled=True)  208 us
    psum x1, waiting for transfers between devices, to_source(): lax.psum(partial_value.astype(jnp.bfloat16), 'mp').astype(jnp.float32)  194 us
    all_gather x1, blocking collectives, on_device(): lax.all_gather(router_weight.astype(jnp.bfloat16), 'expert', axis=0, tile...  140 us
    unnamed x2, blocking collectives  78.1 us
    reduce_scatter x1, waiting for transfers between devices, on_device(): lax.psum_scatter(project_grad, 'expert', scatter_dimension=0, tiled=True)  70.7 us
    all_to_all x2, waiting for transfers between devices, to_owner(): lax.all_to_all(buffer, 'expert', split_axis=0, concat_axis=0, tiled=True)  70.3 us
    psum x2, waiting for transfers between devices, heads_total(): lax.psum(partial_value.astype(jnp.bfloat16), 'mp').astype(jnp.float32)  52.4 us
    all_gather x1, blocking collectives, on_device(): lax.all_gather(norm_gains, ('expert', 'mp'), axis=1, tiled=True)  43.3 us
  transfers between devices with their start and end apart: 10, of which 9 were waited for; matrix products, arithmetic and copies ran while one was open for 12% of the time, Pallas kernels for 0%

commit v1 on v0

v1 whole, which is shorter than its diff:
```python
import functools

import jax
import jax.numpy as jnp
from jax import lax
from jax.experimental import pallas as pl
from jax.experimental.pallas import tpu as pltpu
from jax.sharding import PartitionSpec as P

HEAD = 64
SEQ = 197
MESH = pl.DeviceIdType.MESH
BF = jnp.bfloat16
F32 = jnp.float32
NARROW = 4
LIMIT = 62 * 1024 * 1024
eps_norm = 1e-06


def round_up(value, step):
    return -(-value // step) * step


def norm_parts(value):
    mean_value = jnp.mean(value, axis=-1, keepdims=True)
    centred = value - mean_value
    variance = jnp.mean(centred * centred, axis=-1, keepdims=True)
    inverse = lax.rsqrt(variance + eps_norm)
    return centred * inverse, inverse


def dot_nn(a, b):
    return jnp.dot(a, b, preferred_element_type=F32)


def dot_nt(a, b):
    return lax.dot_general(a, b, (((1,), (1,)), ((), ())), preferred_element_type=F32)


def dot_tn(a, b):
    return lax.dot_general(a, b, (((0,), (0,)), ((), ())), preferred_element_type=F32)


def places():
    e, m = lax.axis_index("expert"), lax.axis_index("mp")
    c, y = lax.rem(m, 2), lax.div(m, 2)
    return e, m, c, y, m + 1 - 2 * c, lax.rem(m + 2, NARROW)


def greet(n, e, m, narrow):
    barrier = pltpu.get_barrier_semaphore()

    def wide(i, carry):
        pl.semaphore_signal(
            barrier, inc=1, device_id={"expert": lax.rem(e + i, n), "mp": m}, device_id_type=MESH
        )
        return carry

    lax.fori_loop(1, n, wide, 0)
    for other in narrow:
        pl.semaphore_signal(
            barrier, inc=1, device_id={"expert": e, "mp": other}, device_id_type=MESH
        )
    pl.semaphore_wait(barrier, n - 1 + len(narrow))


def remote(src, dst, send, recv, e, m):
    return pltpu.make_async_remote_copy(
        src_ref=src,
        dst_ref=dst,
        send_sem=send,
        recv_sem=recv,
        device_id={"expert": e, "mp": m},
        device_id_type=MESH,
    )


def gather_kernel(
    n, mat_ref, vec_ref, mats_ref, tot_ref, first_ref, vmp, vsum, vex, ms, mr, ps, pr, vs, vr
):
    e, m, c, y, sib, far = places()
    greet(n, e, m, [lax.rem(m + j, NARROW) for j in range(1, NARROW)])

    def mat_copy(i, source):
        return remote(mat_ref, mats_ref.at[source], ms.at[i], mr.at[i], lax.rem(e + i, n), m)

    def start_mat(i, carry):
        mat_copy(i, e).start()
        return carry

    lax.fori_loop(1, n, start_mat, 0)
    mats_ref[e] = mat_ref[...]
    narrow = [
        remote(vec_ref, vmp.at[m], ps.at[j], pr.at[j], e, lax.rem(m + j, NARROW))
        for j in range(1, NARROW)
    ]
    for copy in narrow:
        copy.start()
    vmp[m] = vec_ref[...]
    for j in range(1, NARROW):
        remote(
            vec_ref, vmp.at[lax.rem(m + NARROW - j, NARROW)], ps.at[j], pr.at[j], e, m
        ).wait_recv()
    vsum[...] = vmp[0, 0:8] + vmp[1, 0:8] + vmp[2, 0:8] + vmp[3, 0:8]
    for j in range(NARROW):
        first_ref[j] = vmp[j, 8:16]

    def vec_copy(i, source):
        return remote(vsum, vex.at[source], vs.at[i], vr.at[i], lax.rem(e + i, n), m)

    def start_vec(i, carry):
        vec_copy(i, e).start()
        return carry

    lax.fori_loop(1, n, start_vec, 0)
    vex[e] = vsum[...]

    def finish_vec(i, carry):
        vec_copy(i, lax.rem(e + n - i, n)).wait_recv()
        return carry

    lax.fori_loop(1, n, finish_vec, 0)
    tot_ref[...] = vex[0]

    def add_vec(i, carry):
        tot_ref[...] += vex[i]
        return carry

    lax.fori_loop(1, n, add_vec, 0)

    def finish(i, carry):
        mat_copy(i, lax.rem(e + n - i, n)).wait_recv()
        mat_copy(i, e).wait_send()
        vec_copy(i, e).wait_send()
        return carry

    lax.fori_loop(1, n, finish, 0)
    for copy in narrow:
        copy.wait_send()


def gather_params(n, mat, vec):
    width = vec.shape[1]
    sem = pltpu.SemaphoreType.DMA
    return pl.pallas_call(
        functools.partial(gather_kernel, n),
        name="gather_params",
        out_shape=(
            jax.ShapeDtypeStruct((n, *mat.shape), BF),
            jax.ShapeDtypeStruct((8, width), F32),
            jax.ShapeDtypeStruct((NARROW, 8, width), F32),
        ),
        in_specs=[pl.BlockSpec(memory_space=pltpu.VMEM)] * 2,
        out_specs=(pl.BlockSpec(memory_space=pltpu.VMEM),) * 3,
        scratch_shapes=[
            pltpu.VMEM((NARROW, *vec.shape), F32),
            pltpu.VMEM((8, width), F32),
            pltpu.VMEM((n, 8, width), F32),
            sem((n,)),
            sem((n,)),
            sem((NARROW,)),
            sem((NARROW,)),
            sem((n,)),
            sem((n,)),
        ],
        compiler_params=pltpu.CompilerParams(
            collective_id=0, has_side_effects=True, vmem_limit_bytes=LIMIT
        ),
    )(mat, vec)


class Summed:
    def __init__(self, rows, part, sa, sb, tot, sems):
        self.rows, self.part, self.sa, self.sb, self.tot, self.sems = rows, part, sa, sb, tot, sems
        self.e, self.m, self.c, self.y, self.sib, self.far = places()

    def at(self, i):
        return pl.ds(pl.multiple_of(i * self.rows, 16), self.rows)

    def copy_a(self, i):
        at = self.at(i)
        return remote(
            self.part.at[1 - self.c, at],
            self.sa.at[at],
            self.sems.at[0, i],
            self.sems.at[1, i],
            self.e,
            self.sib,
        )

    def copy_b(self, i):
        at = self.at(i)
        return remote(
            self.part.at[self.c, at],
            self.sb.at[at],
            self.sems.at[2, i],
            self.sems.at[3, i],
            self.e,
            self.far,
        )

    def copy_c(self, i, half):
        at = self.at(i)
        return remote(
            self.tot.at[half, at],
            self.tot.at[half, at],
            self.sems.at[4, i],
            self.sems.at[5, i],
            self.e,
            self.sib,
        )

    def start_a(self, i):
        self.copy_a(i).start()

    def step_b(self, i):
        self.copy_a(i).wait_recv()
        at = self.at(i)
        self.part[self.c, at] = (
            self.part[self.c, at].astype(F32) + self.sa[at].astype(F32)
        ).astype(BF)
        self.copy_b(i).start()

    def step_c(self, i):
        self.copy_b(i).wait_recv()
        at = self.at(i)
        self.tot[self.c, at] = (self.part[self.c, at].astype(F32) + self.sb[at].astype(F32)).astype(
            BF
        )
        self.copy_c(i, self.c).start()

    def take(self, i):
        self.copy_c(i, 1 - self.c).wait_recv()
        at = self.at(i)
        return jnp.concatenate([self.tot[0, at].astype(F32), self.tot[1, at].astype(F32)], axis=1)

    def drain(self, images):
        def one(i, carry):
            self.copy_a(i).wait_send()
            self.copy_b(i).wait_send()
            self.copy_c(i, self.c).wait_send()
            return carry

        lax.fori_loop(0, images, one, 0)


def head_masks(width, heads, dtype, value=1.0):
    lane = lax.broadcasted_iota(jnp.int32, (1, width), 1)
    return [
        jnp.where((lane >= h * HEAD) & (lane < (h + 1) * HEAD), value, 0.0).astype(dtype)
        for h in range(heads)
    ]


def forward_kernel(
    n,
    images,
    rows,
    capq,
    x_ref,
    g_ref,
    mats_ref,
    rout_ref,
    vec_ref,
    ab_ref,
    keys_ref,
    routes_ref,
    noise_ref,
    q_ref,
    k_ref,
    v_ref,
    p_ref,
    o_ref,
    h_ref,
    a2_ref,
    gates_ref,
    xr_ref,
    gr_ref,
    gt_ref,
    gb,
    oh,
    xs,
    gs,
    gts,
    wt,
    part,
    sa,
    sb,
    tot,
    ar,
    xss,
    xsr,
    gss,
    gsr,
    tss,
    tsr,
):
    e, m, c, y, sib, far = places()
    count, width = x_ref.shape
    half = width // 2
    lanes = keys_ref.shape[1]
    heads = p_ref.shape[0]
    group = min(4, n)
    stride = NARROW * capq
    greet(n, e, m, [sib, far])
    key0, key1 = keys_ref[0:1, :], keys_ref[1:2, :]

    def dispatch(src, send_buf, recv_buf, ssem, rsem, gates):
        def step(g, carry):
            for j in range(group):
                i = g * group + j
                ex = lax.rem(e + i, n)
                want = lax.broadcasted_iota(jnp.int32, (capq, lanes), 0) + (ex * stride + m * capq)
                hit0, hit1 = key0 == want, key1 == want
                oh[j * capq : (j + 1) * capq, :] = jnp.where(hit0 | hit1, 1.0, 0.0).astype(BF)
                if gates is not None:
                    w = jnp.where(hit0, gates[0], 0.0) + jnp.where(hit1, gates[1], 0.0)
                    ws = w[:, 0:128]
                    for t in range(1, lanes // 128):
                        ws = ws + w[:, t * 128 : (t + 1) * 128]
                    wt[0:capq, :] = ws
                    row = jnp.sum(wt[...].T, axis=0, keepdims=True)
                    gts[i] = jnp.broadcast_to(row, (8, 128))
            block = dot_nn(oh[...], src[...]).astype(BF)
            for j in range(group):
                i = g * group + j
                send_buf[i] = block[j * capq : (j + 1) * capq]

                @pl.when(i == 0)
                def _():
                    recv_buf[e] = send_buf[0]
                    if gates is not None:
                        gt_ref[e] = gts[0]

                @pl.when(i > 0)
                def _():
                    ex = lax.rem(e + i, n)
                    remote(send_buf.at[i], recv_buf.at[e], ssem.at[i], rsem.at[i], ex, m).start()
                    if gates is not None:
                        remote(gts.at[i], gt_ref.at[e], tss.at[i], tsr.at[i], ex, m).start()

            return carry

        lax.fori_loop(0, n // group, step, 0)

    gb[0:count, :] = g_ref[...].astype(BF)
    if lanes > count:
        gb[count:lanes, :] = jnp.zeros((lanes - count, width), BF)
        a2_ref[count:lanes, :] = jnp.zeros((lanes - count, width), BF)
    wt[...] = jnp.zeros_like(wt)
    dispatch(gb, gs, gr_ref, gss, gsr, None)

    summed = Summed(rows, part, sa, sb, tot, ar)
    in_q = head_masks(256, heads, BF, HEAD ** (-0.5))
    in_o = head_masks(256, heads, F32)
    key_ok = lax.broadcasted_iota(jnp.int32, (rows, rows), 1) < SEQ
    gain0, gain1 = vec_ref[0:1, :], vec_ref[1:2, :]
    shift0, shift1 = vec_ref[2:3, :], vec_ref[3:4, :]
    out_shift = vec_ref[6:7, :]

    def attend(i):
        at = summed.at(i)
        normed = (norm_parts(x_ref[at, :].astype(F32))[0] * gain0 + shift0).astype(BF)
        q = (dot_nn(normed, mats_ref[:, 0:256]) + ab_ref[0:1, :]).astype(BF)
        k = dot_nn(normed, mats_ref[:, 256:512]).astype(BF)
        v = (dot_nn(normed, mats_ref[:, 512:768]) + ab_ref[1:2, :]).astype(BF)
        q_ref[at, :], k_ref[at, :], v_ref[at, :] = q, k, v
        o = jnp.zeros((rows, 256), F32)
        for h in range(heads):
            s = jnp.where(key_ok, dot_nt(q * in_q[h], k), -1e30)
            top = jnp.max(s, axis=-1, keepdims=True)
            ex = jnp.exp(s - top)
            p = (ex / jnp.sum(ex, axis=-1, keepdims=True)).astype(BF)
            p_ref[h, at, :] = p
            o = o + dot_nn(p, v) * in_o[h]
        o = o.astype(BF)
        o_ref[at, :] = o
        for hh in range(2):
            part[hh, at] = dot_nt(o, mats_ref[hh * half : (hh + 1) * half, 768:1024]).astype(BF)

    def second(i):
        at = summed.at(i)
        hidden = x_ref[at, :].astype(F32) + summed.take(i) + out_shift
        h_ref[0, at], h_ref[1, at] = hidden[:, :half], hidden[:, half:]
        a2_ref[at, :] = (norm_parts(hidden)[0] * gain1 + shift1).astype(BF)

    def tick(t, carry):
        @pl.when(t < images)
        def _():
            attend(t)
            summed.start_a(t)

        @pl.when((t >= 1) & (t <= images))
        def _():
            summed.step_b(t - 1)

        @pl.when((t >= 3) & (t <= images + 2))
        def _():
            summed.step_c(t - 3)

        @pl.when(t >= 4)
        def _():
            second(t - 4)

        return carry

    lax.fori_loop(0, images + 4, tick, 0)

    logits = dot_nt(rout_ref[...], a2_ref[...]) + noise_ref[...]
    who = lax.broadcasted_iota(jnp.int32, logits.shape, 0)
    picked = [
        jnp.sum(jnp.where(who == routes_ref[kk : kk + 1, :], logits, 0.0), axis=0, keepdims=True)
        for kk in range(2)
    ]
    top = jnp.maximum(picked[0], picked[1])
    ex0, ex1 = jnp.exp(picked[0] - top), jnp.exp(picked[1] - top)
    gate0, gate1 = ex0 / (ex0 + ex1), ex1 / (ex0 + ex1)
    gates_ref[...] = jnp.concatenate([gate0, gate1, jnp.zeros((6, lanes), F32)], axis=0)
    dispatch(a2_ref, xs, xr_ref, xss, xsr, (gate0, gate1))

    def finish(i, carry):
        ex, source = lax.rem(e + i, n), lax.rem(e + n - i, n)
        for send_buf, recv_buf, ssem, rsem in (
            (xs, xr_ref, xss, xsr),
            (gs, gr_ref, gss, gsr),
            (gts, gt_ref, tss, tsr),
        ):
            copy = remote(send_buf.at[i], recv_buf.at[source], ssem.at[i], rsem.at[i], ex, m)
            copy.wait_recv()
            copy.wait_send()
        return carry

    lax.fori_loop(1, n, finish, 0)
    summed.drain(images)


def forward(n, images, rows, capq, heads, x, g, mats, rout, vec, ab, keys, routes, noise):
    count, width = x.shape
    lanes = keys.shape[1]
    half = width // 2
    group = min(4, n)
    sem = pltpu.SemaphoreType.DMA
    struct = jax.ShapeDtypeStruct
    outs = (
        struct((count, 256), BF),
        struct((count, 256), BF),
        struct((count, 256), BF),
        struct((heads, count, rows), BF),
        struct((count, 256), BF),
        struct((2, count, half), F32),
        struct((lanes, width), BF),
        struct((8, lanes), F32),
        struct((n, capq, width), BF),
        struct((n, capq, width), BF),
        struct((n, 8, 128), F32),
    )
    return pl.pallas_call(
        functools.partial(forward_kernel, n, images, rows, capq),
        name="forward",
        out_shape=outs,
        in_specs=[pl.BlockSpec(memory_space=pltpu.VMEM)] * 9,
        out_specs=(pl.BlockSpec(memory_space=pltpu.VMEM),) * len(outs),
        scratch_shapes=[
            pltpu.VMEM((lanes, width), BF),
            pltpu.VMEM((group * capq, lanes), BF),
            pltpu.VMEM((n, capq, width), BF),
            pltpu.VMEM((n, capq, width), BF),
            pltpu.VMEM((n, 8, 128), F32),
            pltpu.VMEM((128, 128), F32),
            pltpu.VMEM((2, count, half), BF),
            pltpu.VMEM((count, half), BF),
            pltpu.VMEM((count, half), BF),
            pltpu.VMEM((2, count, half), BF),
            sem((6, images)),
        ]
        + [sem((n,))] * 6,
        compiler_params=pltpu.CompilerParams(
            collective_id=1, has_side_effects=True, vmem_limit_bytes=LIMIT
        ),
    )(x, g, mats, rout, vec, ab, keys, routes, noise)


def expert_kernel(
    x_ref,
    g_ref,
    gate_ref,
    w1_ref,
    w2_ref,
    b1_ref,
    b2_ref,
    dx_ref,
    gy_ref,
    dg_ref,
    dw1_ref,
    dw2_ref,
    db1_ref,
    db2_ref,
    dy,
    xt,
    yacc,
    dxacc,
):
    step = pl.program_id(0) * pl.num_programs(1) + pl.program_id(1)
    last = pl.num_programs(0) * pl.num_programs(1) - 1

    @pl.when(step == 0)
    def _():
        grad = (g_ref[...].astype(F32) * gate_ref[...]).astype(BF)
        dy[...] = grad
        db2_ref[...] = jnp.broadcast_to(
            jnp.sum(grad.astype(F32), axis=0, keepdims=True), db2_ref.shape
        )
        xt[...] = x_ref[...].T
        yacc[...] = jnp.zeros_like(yacc)
        dxacc[...] = jnp.zeros_like(dxacc)

    w1, w2 = w1_ref[0], w2_ref[0]
    z = dot_nn(x_ref[...], w1) + b1_ref[0, 0:1, :]
    cdf = 0.5 * (1.0 + lax.erf(z * (2.0**-0.5)))
    pdf = jnp.exp(-0.5 * z * z) * ((2.0 * jnp.pi) ** -0.5)
    u = (z * cdf).astype(BF)
    yacc[...] += dot_nn(u, w2)
    dz = dot_nt(dy[...], w2) * (cdf + z * pdf)
    db1_ref[0] = jnp.broadcast_to(
        jnp.sum(dz, axis=0, keepdims=True), (db1_ref.shape[1], dz.shape[1])
    )
    dz = dz.astype(BF)
    dxacc[...] += dot_nt(dz, w1)
    dw2_ref[0] = dot_tn(u, dy[...]).astype(BF)
    dw1_ref[0] = dot_nn(xt[...], dz).astype(BF)

    @pl.when(step == last)
    def _():
        yv = yacc[...] + b2_ref[0:1, :]
        gy_ref[...] = (yv * gate_ref[...]).astype(BF)
        dg_ref[...] = jnp.sum(yv * g_ref[...].astype(F32), axis=1, keepdims=True)
        dx_ref[...] = dxacc[...].astype(BF)


def experts(x, g, gate, w1, w2, b1, b2, chunk):
    slots, width = x.shape
    hidden = w1.shape[2]
    struct = jax.ShapeDtypeStruct
    whole = lambda q, j: (0, 0)
    return pl.pallas_call(
        expert_kernel,
        name="experts",
        grid=(NARROW, hidden // chunk),
        out_shape=(
            struct((slots, width), BF),
            struct((slots, width), BF),
            struct((slots, 1), F32),
            struct(w1.shape, BF),
            struct(w2.shape, BF),
            struct(b1.shape, F32),
            struct((8, width), F32),
        ),
        in_specs=[
            pl.BlockSpec((slots, width), whole),
            pl.BlockSpec((slots, width), whole),
            pl.BlockSpec((slots, 1), whole),
            pl.BlockSpec((1, width, chunk), lambda q, j: (q, 0, j)),
            pl.BlockSpec((1, chunk, width), lambda q, j: (q, j, 0)),
            pl.BlockSpec((1, 8, chunk), lambda q, j: (q, 0, j)),
            pl.BlockSpec((1, width), whole),
        ],
        out_specs=(
            pl.BlockSpec((slots, width), whole),
            pl.BlockSpec((slots, width), whole),
            pl.BlockSpec((slots, 1), whole),
            pl.BlockSpec((1, width, chunk), lambda q, j: (q, 0, j)),
            pl.BlockSpec((1, chunk, width), lambda q, j: (q, j, 0)),
            pl.BlockSpec((1, 8, chunk), lambda q, j: (q, 0, j)),
            pl.BlockSpec((8, width), whole),
        ),
        scratch_shapes=[
            pltpu.VMEM((slots, width), BF),
            pltpu.VMEM((width, slots), BF),
            pltpu.VMEM((slots, width), F32),
            pltpu.VMEM((slots, width), F32),
        ],
        compiler_params=pltpu.CompilerParams(vmem_limit_bytes=LIMIT),
    )(x, g, gate, w1, w2, b1, b2)


def backward_kernel(
    n,
    images,
    rows,
    capq,
    lanes_each,
    direct,
    dx_ref,
    gy_ref,
    dg_ref,
    x_ref,
    g_ref,
    h_ref,
    q_ref,
    k_ref,
    v_ref,
    p_ref,
    o_ref,
    a2_ref,
    gates_ref,
    keys_ref,
    routes_ref,
    mats_ref,
    rpad_ref,
    vec_ref,
    db_ref,
    fg_ref,
    po_ref,
    pg_ref,
    small_ref,
    dbo_ref,
    dxr,
    gyr,
    dgr,
    oht,
    dlog,
    part,
    sa,
    sb,
    tot,
    dh,
    part2,
    tot2,
    sa2,
    sb2,
    dq,
    dk,
    dv,
    dr,
    a1,
    acc,
    mine,
    mpv,
    exv,
    pgs,
    pgr,
    ar,
    ar2,
    pss,
    dxs,
    dxv,
    gys,
    gyv,
    dgs,
    dgv,
    pgss,
    pgsr,
    mss,
    msr,
    ess,
    esr,
):
    e, m, c, y, sib, far = places()
    count, width = x_ref.shape
    half = width // 2
    heads = p_ref.shape[0]
    stride = NARROW * capq
    slots = n * lanes_each
    span = lanes_each if lanes_each >= 128 else 128
    per = 128 // lanes_each if lanes_each < 128 else 1
    experts_pad = acc.shape[0] - 8
    here = pl.ds(0, capq)
    if lanes_each > capq:
        for buf in (dxr, gyr):
            buf[:, capq:lanes_each, :] = jnp.zeros((n, lanes_each - capq, width), BF)
    greet(n, e, m, [lax.rem(m + j, NARROW) for j in range(1, NARROW)])

    def dx_copy(i, to, source):
        return remote(dx_ref.at[to], dxr.at[source, here], dxs.at[i], dxv.at[i], to, m)

    def dg_copy(i, to, source):
        return remote(dg_ref.at[to], dgr.at[source], dgs.at[i], dgv.at[i], to, m)

    def gy_copy(i, to, source):
        return remote(gy_ref.at[to], gyr.at[source, here], gys.at[i], gyv.at[i], to, m)

    def start_dx(i, carry):
        to = lax.rem(e + i, n)
        dx_copy(i, to, e).start()
        dg_copy(i, to, e).start()
        return carry

    def start_gy(i, carry):
        gy_copy(i, lax.rem(e + i, n), e).start()
        return carry

    lax.fori_loop(1, n, start_dx, 0)
    lax.fori_loop(1, n, start_gy, 0)
    dxr[e, 0:capq, :] = dx_ref[e]
    gyr[e, 0:capq, :] = gy_ref[e]
    dgr[e] = dg_ref[e]

    gain0, gain1 = vec_ref[0:1, :], vec_ref[1:2, :]
    shift0 = vec_ref[2:3, :]

    lane = lax.broadcasted_iota(jnp.int32, (1, slots), 1)
    place = lane % lanes_each
    want = (lane // lanes_each) * stride + place + m * capq
    want = jnp.where(place < capq, want, -2)

    def fill(i, carry):
        at = pl.ds(pl.multiple_of(i * rows, 16), rows)
        hit = (keys_ref[at, 0:1] == want) | (keys_ref[at, 1:2] == want)
        oht[at, :] = jnp.where(hit, 1.0, 0.0).astype(BF)
        return carry

    lax.fori_loop(0, images, fill, 0)
    acc[...] = jnp.zeros_like(acc)

    def arrive_dx(i, carry):
        source = lax.rem(e + n - i, n)
        dx_copy(i, source, source).wait_recv()
        dg_copy(i, source, source).wait_recv()
        return carry

    lax.fori_loop(1, n, arrive_dx, 0)
    pieces = []
    for block in range(n // per):
        piece = dgr[block * per]
        for j in range(1, per):
            piece = piece + dgr[block * per + j]
        pieces.append(piece[0:1, :])
    dgrow = jnp.concatenate(pieces, axis=1)

    summed = Summed(rows, part, sa, sb, tot, ar)
    again = Summed(rows, part2, sa2, sb2, tot2, ar2)
    rlane = lax.broadcasted_iota(jnp.int32, (1, rpad_ref.shape[0]), 1)

    def returned(i):
        at = summed.at(i)
        dgate = [
            jnp.sum(jnp.where(keys_ref[at, kk : kk + 1] == want, dgrow, 0.0), axis=1, keepdims=True)
            for kk in range(2)
        ]
        gate0, gate1 = gates_ref[at, 0:1], gates_ref[at, 1:2]
        mean = gate0 * dgate[0] + gate1 * dgate[1]
        dl = jnp.where(routes_ref[at, 0:1] == rlane, gate0 * (dgate[0] - mean), 0.0)
        dl = dl + jnp.where(routes_ref[at, 1:2] == rlane, gate1 * (dgate[1] - mean), 0.0)
        dl = dl.astype(BF)
        dlog[at, :] = dl
        for hh in range(2):
            cols = slice(hh * half, (hh + 1) * half)
            rowsum = dot_nn(oht[at, :], dxr[:, :, cols].reshape(slots, half))
            part[hh, at] = (rowsum + dot_nn(dl, rpad_ref[:, cols])).astype(BF)

    in_b = head_masks(256, heads, BF)
    in_f = head_masks(256, heads, F32)
    scale = HEAD ** (-0.5)

    def attend(i):
        at = summed.at(i)
        da2 = summed.take(i)
        hidden = jnp.concatenate([h_ref[0, at], h_ref[1, at]], axis=1)
        normed, inverse = norm_parts(hidden)
        mixed = da2 * normed
        acc[1:2, :] += jnp.sum(mixed, axis=0, keepdims=True)
        acc[3:4, :] += jnp.sum(da2, axis=0, keepdims=True)
        mean_mixed = jnp.mean(mixed * gain1, axis=-1, keepdims=True)
        g2 = da2 * gain1
        mean_grad = jnp.mean(g2, axis=-1, keepdims=True)
        grad = g_ref[at, :] + inverse * (g2 - mean_grad - normed * mean_mixed)
        dh[at, :] = grad
        acc[6:7, :] += jnp.sum(grad, axis=0, keepdims=True)
        low = grad.astype(BF)
        dr[at, :] = low
        do = dot_nn(low, mats_ref[:, 768:1024]).astype(BF)
        q, k, v = q_ref[at, :], k_ref[at, :], v_ref[at, :]
        zero = jnp.zeros((rows, 256), F32)
        dqa, dka, dva = zero, zero, zero
        for h in range(heads):
            p = p_ref[h, at, :]
            dp = dot_nt(do * in_b[h], v)
            pf = p.astype(F32)
            t = pf * dp
            ds = (t - pf * jnp.sum(t, axis=-1, keepdims=True)).astype(BF)
            dqa = dqa + dot_nn(ds, k) * in_f[h]
            dka = dka + dot_tn(ds, q) * in_f[h]
            dva = dva + dot_tn(p, do) * in_f[h]
        dqb, dkb, dvb = (dqa * scale).astype(BF), (dka * scale).astype(BF), dva.astype(BF)
        dq[at, :], dk[at, :], dv[at, :] = dqb, dkb, dvb
        acc[4:5, 0:256] += jnp.sum(dqb.astype(F32), axis=0, keepdims=True)
        acc[5:6, 0:256] += jnp.sum(dvb.astype(F32), axis=0, keepdims=True)
        for hh in range(2):
            r = slice(hh * half, (hh + 1) * half)
            part2[hh, at] = (
                dot_nt(dqb, mats_ref[r, 0:256])
                + dot_nt(dkb, mats_ref[r, 256:512])
                + dot_nt(dvb, mats_ref[r, 512:768])
            ).astype(BF)

    def last(i):
        at = again.at(i)
        da1 = again.take(i)
        normed, inverse = norm_parts(x_ref[at, :].astype(F32))
        a1[at, :] = (normed * gain0 + shift0).astype(BF)
        mixed = da1 * normed
        acc[0:1, :] += jnp.sum(mixed, axis=0, keepdims=True)
        acc[2:3, :] += jnp.sum(da1, axis=0, keepdims=True)
        mean_mixed = jnp.mean(mixed * gain0, axis=-1, keepdims=True)
        g1 = da1 * gain0
        mean_grad = jnp.mean(g1, axis=-1, keepdims=True)
        fg_ref[at, :] = dh[at, :] + inverse * (g1 - mean_grad - normed * mean_mixed)

    def tick(t, carry):
        @pl.when(t < images)
        def _():
            returned(t)
            summed.start_a(t)

        @pl.when((t >= 1) & (t <= images))
        def _():
            summed.step_b(t - 1)

        @pl.when((t >= 3) & (t <= images + 2))
        def _():
            summed.step_c(t - 3)

        @pl.when((t >= 4) & (t <= images + 3))
        def _():
            attend(t - 4)
            again.start_a(t - 4)

        @pl.when((t >= 5) & (t <= images + 4))
        def _():
            again.step_b(t - 5)

        @pl.when((t >= 7) & (t <= images + 6))
        def _():
            again.step_c(t - 7)

        @pl.when(t >= 8)
        def _():
            last(t - 8)

        return carry

    lax.fori_loop(0, images + 8, tick, 0)
    summed.drain(images)
    again.drain(images)

    def arrive_gy(i, carry):
        source = lax.rem(e + n - i, n)
        gy_copy(i, source, source).wait_recv()
        return carry

    lax.fori_loop(1, n, arrive_gy, 0)

    def combine(i, carry):
        at = summed.at(i)
        for hh in range(2):
            cols = slice(hh * half, (hh + 1) * half)
            part[hh, at] = dot_nn(oht[at, :], gyr[:, :, cols].reshape(slots, half)).astype(BF)
        return carry

    lax.fori_loop(0, images, combine, 0)
    both = count // 2
    own = pl.ds(pl.multiple_of(c * both, 16), both)
    other = pl.ds(pl.multiple_of((1 - c) * both, 16), both)
    low_half, high_half = pl.ds(0, both), pl.ds(both, both)
    copy_pa = [
        remote(
            part.at[hh, other], sa.at[pl.ds(hh * both, both)], pss.at[hh], pss.at[2 + hh], e, sib
        )
        for hh in range(2)
    ]
    for copy in copy_pa:
        copy.start()
    for copy in copy_pa:
        copy.wait_recv()
    for hh in range(2):
        sb2[hh * both : (hh + 1) * both] = (
            part[hh, own].astype(F32) + sa[hh * both : (hh + 1) * both].astype(F32)
        ).astype(BF)
    send_to = pl.ds(pl.multiple_of((1 - y) * both, 16), both)
    keep_at = pl.ds(pl.multiple_of(y * both, 16), both)
    copy_pb = remote(sb2.at[send_to], sa2.at[low_half], pss.at[4], pss.at[5], e, far)
    copy_pb.start()

    pgs_full = [
        (a1, dq),
        (a1, dk),
        (a1, dv),
        (dr, o_ref),
    ]
    quarter = heads * HEAD
    for slot, (left, right) in enumerate(pgs_full):
        grad = dot_tn(left[...], right[...])[:, :quarter].astype(BF)
        cols = slice(slot * quarter, (slot + 1) * quarter)
        if direct:
            for i in range(n):
                pgs[i, :, cols] = grad[i * (width // n) : (i + 1) * (width // n)]
        else:
            pg_ref[:, cols] = grad.astype(F32)
    router_grad = dot_tn(dlog[...], a2_ref[0:count, :])
    acc[8 : 8 + experts_pad, :] = router_grad[0:experts_pad]

    if direct:

        def pg_copy(i, to, source):
            return remote(pgs.at[to], pgr.at[source], pgss.at[i], pgsr.at[i], to, m)

        def start_pg(i, carry):
            pg_copy(i, lax.rem(e + i, n), e).start()
            return carry

        lax.fori_loop(1, n, start_pg, 0)
        pgr[e] = pgs[e]

    wide = acc.shape[0]
    lane_w = lax.broadcasted_iota(jnp.int32, (1, width), 1)
    own_cols = (lane_w >= m * quarter) & (lane_w < (m + 1) * quarter)
    mine[0:8, :] = jnp.where(own_cols, acc[0:8, :], 0.0)
    mine[8:wide, :] = acc[8:wide, :]
    mine[wide:, :] = db_ref[...]
    bias = acc[4:6, 0:quarter]
    mine[4:6, :] = jnp.zeros((2, width), F32)
    for mm in range(NARROW):

        @pl.when(m == mm)
        def _():
            mine[4:6, mm * quarter : (mm + 1) * quarter] = bias

    narrow = [
        remote(mine, mpv.at[m], mss.at[j], msr.at[j], e, lax.rem(m + j, NARROW))
        for j in range(1, NARROW)
    ]
    for copy in narrow:
        copy.start()
    mpv[m] = mine[...]
    for j in range(1, NARROW):
        remote(
            mine, mpv.at[lax.rem(m + NARROW - j, NARROW)], mss.at[j], msr.at[j], e, m
        ).wait_recv()
    sums = mpv[0] + mpv[1] + mpv[2] + mpv[3]
    dbo_ref[...] = sums[wide:]
    small_ref[...] = sums[0:wide]
    acc[...] = sums[0:wide]

    top = pl.ds(0, exv.shape[1])

    def ex_copy(i, to, source):
        return remote(acc.at[top], exv.at[source], ess.at[i], esr.at[i], to, m)

    def start_ex(i, carry):
        ex_copy(i, lax.rem(e + i, n), e).start()
        return carry

    lax.fori_loop(1, n, start_ex, 0)

    copy_pb.wait_recv()
    yy = pl.ds(0, both)
    total = sb2[keep_at].astype(F32) + sa2[yy].astype(F32) + h_ref[y, own]
    po_ref[own, :] = total.astype(BF)
    copy_pc = remote(po_ref.at[own], po_ref.at[own], pss.at[6], pss.at[7], e, sib)
    copy_pc.start()
    wait_pc = remote(po_ref.at[other], po_ref.at[other], pss.at[6], pss.at[7], e, sib)

    def finish_ex(i, carry):
        source = lax.rem(e + n - i, n)
        ex_copy(i, source, source).wait_recv()
        small_ref[top, :] += exv[source]
        return carry

    lax.fori_loop(1, n, finish_ex, 0)
    wait_pc.wait_recv()

    if direct:

        def finish_pg(i, carry):
            source = lax.rem(e + n - i, n)
            pg_copy(i, source, source).wait_recv()
            return carry

        lax.fori_loop(1, n, finish_pg, 0)
        total = pgr[0].astype(F32)
        for i in range(1, n):
            total = total + pgr[i].astype(F32)
        pg_ref[...] = total

    def drain(i, carry):
        to = lax.rem(e + i, n)
        dx_copy(i, to, e).wait_send()
        dg_copy(i, to, e).wait_send()
        gy_copy(i, to, e).wait_send()
        ex_copy(i, to, e).wait_send()
        if direct:
            pg_copy(i, to, e).wait_send()
        return carry

    lax.fori_loop(1, n, drain, 0)
    for copy in copy_pa + [copy_pb, copy_pc] + narrow:
        copy.wait_send()


def backward(n, images, rows, capq, lanes_each, direct, extra, *args):
    dx, x, p = args[0], args[3], args[9]
    count, width = x.shape
    half = width // 2
    heads = p.shape[0]
    quarter = heads * HEAD
    slots = n * lanes_each
    each = width // n
    sem = pltpu.SemaphoreType.DMA
    struct = jax.ShapeDtypeStruct
    wide = 8 + extra
    tail = args[-1].shape[0]
    outs = (
        struct((count, width), F32),
        struct((count, half), BF),
        struct((each if direct else width, 4 * quarter), F32),
        struct((wide, width), F32),
        struct((tail, width), F32),
    )
    block = (n, each, 4 * quarter) if direct else (1, 16, 128)
    return pl.pallas_call(
        functools.partial(backward_kernel, n, images, rows, capq, lanes_each, direct),
        name="backward",
        out_shape=outs,
        in_specs=[pl.BlockSpec(memory_space=pltpu.VMEM)] * len(args),
        out_specs=(pl.BlockSpec(memory_space=pltpu.VMEM),) * len(outs),
        scratch_shapes=[
            pltpu.VMEM((n, lanes_each, width), BF),
            pltpu.VMEM((n, lanes_each, width), BF),
            pltpu.VMEM((n, 8, 128), F32),
            pltpu.VMEM((count, slots), BF),
            pltpu.VMEM((count, 128), BF),
            pltpu.VMEM((2, count, half), BF),
            pltpu.VMEM((count, half), BF),
            pltpu.VMEM((count, half), BF),
            pltpu.VMEM((2, count, half), BF),
            pltpu.VMEM((count, width), F32),
            pltpu.VMEM((2, count, half), BF),
            pltpu.VMEM((2, count, half), BF),
            pltpu.VMEM((count, half), BF),
            pltpu.VMEM((count, half), BF),
            pltpu.VMEM((count, 256), BF),
            pltpu.VMEM((count, 256), BF),
            pltpu.VMEM((count, 256), BF),
            pltpu.VMEM((count, width), BF),
            pltpu.VMEM((count, width), BF),
            pltpu.VMEM((wide, width), F32),
            pltpu.VMEM((wide + tail, width), F32),
            pltpu.VMEM((NARROW, wide + tail, width), F32),
            pltpu.VMEM((n, wide if direct else 8, width), F32),
            pltpu.VMEM(block, BF),
            pltpu.VMEM(block, BF),
            sem((6, images)),
            sem((6, images)),
            sem((8,)),
        ]
        + [sem((n,))] * 8
        + [sem((NARROW,))] * 2
        + [sem((n,))] * 2,
        compiler_params=pltpu.CompilerParams(
            collective_id=2, has_side_effects=True, vmem_limit_bytes=LIMIT
        ),
    )(*args)


def on_device(
    features,
    norm_gains,
    norm_shifts,
    attention_bias,
    output_bias,
    project_weight,
    merge_weight,
    router_weight,
    router_noise,
    routes,
    slot_numbers,
    expand_weight,
    expand_bias,
    contract_weight,
    contract_bias,
    cotangent,
):
    count, width = features.shape
    n = lax.axis_size("expert")
    e, m = lax.axis_index("expert"), lax.axis_index("mp")
    capacity = 3 * count // n
    quarter = project_weight.shape[2]
    heads = quarter // HEAD
    images = count // SEQ
    rows = round_up(SEQ, 16)
    padded = images * rows
    lanes = round_up(padded, 128)
    capq = round_up(-(-capacity // NARROW), 16)
    lanes_each = 16
    while lanes_each < capq:
        lanes_each *= 2
    each = width // n
    direct = each % 16 == 0
    owners = router_weight.shape[1]
    extra = round_up(owners, 8)

    low = project_weight.astype(BF)
    gap = jnp.zeros((each, 256 - quarter), BF)
    router_gap = jnp.zeros((each, 256 - quarter - owners), BF)
    mat = jnp.concatenate(
        [
            low[:, 0],
            router_weight.astype(BF),
            router_gap,
            low[:, 1],
            gap,
            low[:, 2],
            gap,
            merge_weight.T.astype(BF),
            gap,
        ],
        axis=1,
    )
    share = norm_gains.shape[1]
    packed = jnp.concatenate(
        [norm_gains, norm_shifts, attention_bias, output_bias[None], jnp.zeros((1, share), F32)]
    )
    vec = jnp.zeros((8, width), F32)
    vec = lax.dynamic_update_slice_in_dim(vec, packed, (e * NARROW + m) * share, 1)
    vec = jnp.concatenate([vec, jnp.broadcast_to(expand_bias, (8, width))])
    mats, vecs, first_bias = gather_params(n, mat, vec)
    mats = mats.reshape(width, 1024)
    router_t = mats[:, quarter : quarter + owners].T
    router_fwd = jnp.pad(router_t, ((0, extra - owners), (0, 0)))
    router_bwd = jnp.pad(router_t, ((0, 128 - owners), (0, 0)))
    ab = lax.dynamic_slice_in_dim(vecs[4:6], m * quarter, quarter, 1)
    ab = jnp.pad(ab, ((0, 6), (0, 256 - quarter)))

    def pad_rows(value, fill=0):
        value = value.reshape(images, SEQ, value.shape[1])
        return jnp.pad(value, ((0, 0), (0, rows - SEQ), (0, 0)), constant_values=fill).reshape(
            padded, -1
        )

    def along_lanes(value, top, fill=0):
        return jnp.pad(
            value.T,
            ((0, top - value.shape[1]), (0, lanes - padded)),
            constant_values=fill,
        )

    x = pad_rows(features)
    g = pad_rows(cotangent)
    keys = pad_rows(routes * (NARROW * capq) + slot_numbers, -1)
    routes_col = pad_rows(routes)
    noise = pad_rows(router_noise)
    w1 = lax.all_gather(expand_weight[0].astype(BF), "mp", axis=0)
    w2 = lax.all_gather(contract_weight[0].astype(BF), "mp", axis=0)
    q, k, v, p, o, h, a2, gates, xr, gr, gt = forward(
        n,
        images,
        rows,
        capq,
        heads,
        x,
        g,
        mats,
        router_fwd,
        vecs,
        ab,
        along_lanes(keys, 8, -1),
        along_lanes(routes_col, 8),
        along_lanes(noise, extra),
    )
    slots = n * capq
    gate_col = gt[:, 0, :capq].reshape(slots, 1)
    dx, gy, dg, dw1, dw2, db1, db2 = experts(
        xr.reshape(slots, width),
        gr.reshape(slots, width),
        gate_col,
        w1,
        w2,
        first_bias,
        contract_bias,
        256,
    )
    expand_grad = lax.psum_scatter(dw1, "mp", scatter_dimension=0)
    contract_grad = lax.psum_scatter(dw2, "mp", scatter_dimension=0)
    dg = jnp.pad(dg.reshape(n, capq), ((0, 0), (0, 128 - capq)))
    dg = jnp.roll(dg, (e * lanes_each) % 128, axis=1)
    dg = jnp.broadcast_to(dg[:, None, :], (n, 8, 128))
    db = jnp.concatenate([db1[:, 0], db2[0:1], jnp.zeros((3, width), F32)])
    fg, po, pg, small, dbo = backward(
        n,
        images,
        rows,
        capq,
        lanes_each,
        direct,
        extra,
        dx.reshape(n, capq, width),
        gy.reshape(n, capq, width),
        dg,
        x,
        g,
        h,
        q,
        k,
        v,
        p,
        o,
        a2,
        gates.T,
        keys,
        routes_col,
        mats,
        router_bwd,
        vecs,
        db,
    )

    def unpad(value):
        return value.reshape(images, rows, -1)[:, :SEQ].reshape(count, -1)

    block_output = lax.dynamic_slice_in_dim(unpad(po), lax.rem(m, 2) * quarter, quarter, 1)
    if not direct:
        pg = lax.psum_scatter(pg, "expert", scatter_dimension=0, tiled=True)
    project_share = pg[:, : 3 * quarter].reshape(each, 3, quarter)
    merge_share = pg[:, 3 * quarter :].T
    mine = lax.dynamic_slice_in_dim(small[0:8], (e * NARROW + m) * share, share, 1)
    router_rows = small[8 : 8 + owners]
    if not direct:
        router_rows = lax.psum(router_rows, "expert")
    router_share = lax.dynamic_slice_in_dim(router_rows, e * each, each, 1).T
    return (
        block_output,
        unpad(fg),
        mine[0:2],
        mine[2:4],
        mine[4:6],
        mine[6],
        project_share,
        merge_share,
        router_share,
        expand_grad[None].astype(F32),
        lax.dynamic_slice_in_dim(dbo, m, 1, 0),
        contract_grad[None].astype(F32),
        dbo[4:5],
    )


def solution(mesh):
    placed = (
        P("expert", None),
        P(None, ("expert", "mp")),
        P(None, ("expert", "mp")),
        P(None, ("expert", "mp")),
        P(("expert", "mp")),
        P("expert", None, "mp"),
        P("mp", "expert"),
        P("expert", None),
        P("expert", None),
        P("expert", None),
        P("expert", None),
        P("expert", None, "mp"),
        P("expert", "mp"),
        P("expert", "mp", None),
        P("expert", None),
        P("expert", None),
    )
    return jax.shard_map(
        on_device,
        mesh=mesh,
        in_specs=placed,
        out_specs=(
            P("expert", "mp"),
            P("expert", None),
            P(None, ("expert", "mp")),
            P(None, ("expert", "mp")),
            P(None, ("expert", "mp")),
            P(("expert", "mp")),
            P("expert", None, "mp"),
            P("mp", "expert"),
            P("expert", None),
            P("expert", None, "mp"),
            P("expert", "mp"),
            P("expert", "mp", None),
            P("expert", None),
        ),
        check_vma=False,
    )
```

time: 1470 us -> 405 us (0.28)
  waiting for transfers between devices: 628 us -> 0.54 us
  blocking collectives: 408 us -> 0 us
  Pallas kernels: 0 us -> 336 us
  local copies, waits for them, and re-layouts: 187 us -> 40.3 us
  matrix products: 111 us -> 0 us
  other arithmetic: 91.9 us -> 11.4 us
  starting transfers between devices: 21 us -> 0.16 us
    pallas_call x0 -> x4, Pallas kernels: none -> 336 us  [the longest x1 172 us: backward(): pl.pallas_call(functools.partial(backward_kernel, n, images, rows, capq,...]
    all_gather x6 -> x0, blocking collectives: 330 us -> none  [the longest x1 140 us: on_device(): lax.all_gather(router_weight.astype(jnp.bfloat16), 'expert', axis=0, tile...]
    all_to_all x4 -> x0, waiting for transfers between devices: 278 us -> none  [the longest x2 208 us: to_source(): lax.all_to_all(rounded, 'expert', split_axis=0, concat_axis=0, tiled=True)]
    psum x3 -> x0, waiting for transfers between devices: 246 us -> none  [the longest x1 194 us: to_source(): lax.psum(partial_value.astype(jnp.bfloat16), 'mp').astype(jnp.float32)]
    dot_general x19 -> x0, matrix products: 105 us -> none  [the longest x1 31.2 us: on_device(): jnp.dot(arrived, expand_low, preferred_element_type=jnp.float32)]
    unnamed x2 -> x0, blocking collectives: 78.1 us -> none
    reduce_scatter x1 -> x2, waiting for transfers between devices: 70.7 us -> 0.01 us  [the longest x1 0.01 us: on_device(): expand_grad = lax.psum_scatter(dw1, 'mp', scatter_dimension=0)]
    reshape x11 -> x9, local copies, waits for them, and re-layouts: 62.4 us -> 11.3 us  [the longest x5 6.51 us: pad_rows(): value = value.reshape(images, SEQ, value.shape[1])]
  transfers between devices with their start and end apart: 10 -> 4, of which waited for: 9 -> 0; matrix products, arithmetic and copies ran while one was open for 12% -> 11% of each run, Pallas kernels for 0% -> 71%
where the time goes in v1:
time: 405 us; the launch traced here: 403 us
  Pallas kernels  336 us (83%)
  local copies, waits for them, and re-layouts  40.3 us (10%)
  between operations  14.3 us (4%)
  other arithmetic  11.4 us (3%)
    pallas_call x1, Pallas kernels, backward(): pl.pallas_call(functools.partial(backward_kernel, n, images, rows, capq,...  172 us
    pallas_call x1, Pallas kernels, forward(): pl.pallas_call(functools.partial(forward_kernel, n, images, rows, capq),...  67.8 us
    pallas_call x1, Pallas kernels, experts(): pl.pallas_call(expert_kernel, name='experts', grid=(NARROW, hidden // chu...  49.6 us
    pallas_call x1, Pallas kernels, gather_params(): pl.pallas_call(functools.partial(gather_kernel, n), name='gather_params',...  47.1 us
  transfers between devices with their start and end apart: 4, of which 0 were waited for; matrix products, arithmetic and copies ran while one was open for 11% of the time, Pallas kernels for 71%

profile of v1, /device:TPU:0, one launch (start us, length us, event | category | flops | bytes accessed | tf_op | source)
XLA Modules:
  0.0 402.7 jit_solution(14975680263288850020)
XLA Ops:
  7.2 2.9 convert_element_type.44
  10.4 1.1 convert_element_type.45
  12.3 0.8 concatenate.16.mat_ref
  13.7 47.1 %gather_params.1 = (bf16[8,96,1024]{2,1,0:T(8,128)(2,1)}, f32[8,768]{1,0:T(8,128)}, f32[4,8,768]{2,1,0:T(8,128)}) custom-call(bf16[96,1024]{1,0:T(8,128)(2,1)} %concatenate.16.mat_ref, f32[16,768]{1,0:T(8,128)} %pad_maximum_fusion.vec_ref), custom_call_target="tpu_custom_call" | custom-call | tf_op jit(solution)/shard_map/gather_params/pallas_call | solution.py:145
  60.8 0.7 slice.61
  62.2 1.1 slice.79
  64.0 4.3 %reshape.92 = f32[6,197,768]{2,1,0:T(8,128)} reshape(f32[1182,768]{1,0:T(8,128)} %param.31) | data formatting | bytes 7262208 | tf_op jit(solution)/shard_map/reshape | solution.py:1135
  68.3 4.3 %pad.43 = f32[6,208,768]{2,1,0:T(8,128)} pad(f32[6,197,768]{2,1,0:T(8,128)} %reshape.92, f32[]{:T(128)} %constant.27.clone.1), padding=0_0x0_11x0_0 | pad | bytes 7464964 | tf_op jit(solution)/shard_map/jit(_pad)/pad | solution.py:1136
  72.6 2.0 reshape.90
  74.6 1.4 pad.42
  79.4 67.8 %forward.1 = (bf16[1248,256]{1,0:T(8,128)(2,1)}, bf16[1248,256]{1,0:T(8,128)(2,1)}, bf16[1248,256]{1,0:T(8,128)(2,1)}, bf16[3,1248,208]{2,1,0:T(8,128)(2,1)}, bf...) custom-call(bf16[1248,768]{1,0:T(8,128)(2,1)} %bitcast.47, ...), custom_call_target="tpu_custom_call" | custom-call | tf_op jit(solution)/shard_map/forward/pallas_call | solution.py:457
  147.2 0.8 slice_reduce_fusion
  148.0 1.0 reshape_squeeze.4.gate_ref
  149.0 49.6 %experts.1 = (bf16[896,768]{1,0:T(8,128)(2,1)}, bf16[896,768]{1,0:T(8,128)(2,1)}, f32[896,1]{1,0:T(8,128)}, bf16[4,768,768]{2,1,0:T(8,128)(2,1)}, bf16[4,768,768...) custom-call(bf16[896,768]{1,0:T(8,128)(2,1)} %bitcast.60, bf16[896,768]{1,0:T(8,128)(2,1)} %bitcast.61, ...), custom_call_target="tpu_custom_call" | custom-call | tf_op jit(solution)/shard_map/experts/pallas_call | solution.py:545
  200.1 1.1 copy.65
  203.7 171.5 %backward.1 = (f32[1248,768]{1,0:T(8,128)}, bf16[1248,384]{1,0:T(8,128)(2,1)}, f32[96,768]{1,0:T(8,128)}, f32[16,768]{1,0:T(8,128)}, f32[8,768]{1,0:T(8,128)}) custom-call(bf16[8,112,768]{2,1,0:T(8,128)(2,1)} %bitcast.58, bf16[8,112,768]{2,1,0:T(8,128)(2,1)} %bitcast.59, f32[8,8,128]{2,1,0:T(8,128)} %broadcast_in_dim.34.dg_ref, bf16[1248,768]{1,0:T(8,128)(2,1)} %bitcast.48, ...), custom_call_target="tpu_custom_call" | custom-call | tf_op jit(solution)/shard_map/backward/pallas_call | solution.py:1020
  375.2 4.1 %slice.82 = f32[6,197,768]{2,1,0:T(8,128)} slice(f32[6,208,768]{2,1,0:T(8,128)} %bitcast.56), slice={[0:6], [0:197], [0:768]} | slice | bytes 7262208 | tf_op jit(solution)/shard_map/slice | solution.py:1218
  379.3 4.4 %reshape.109 = f32[1182,768]{1,0:T(8,128)} reshape(f32[6,197,768]{2,1,0:T(8,128)} %slice.82) | data formatting | bytes 7262208 | tf_op jit(solution)/shard_map/reshape | solution.py:1218
  384.3 1.0 copy.68
  385.5 0.9 copy.69
  386.5 0.7 copy.70
  389.1 1.4 fusion.2
  390.5 2.8 convert_element_type.46
  393.3 2.8 convert_element_type.47
  (109 shorter events, 12.8 us)
Async XLA Ops:
  7.2 3.2 copy-start.2
  7.2 141.8 %all-gather.3.cloned.1.call-start = ((), (), s32[]{:S(2)}) async-start(), calls=%async_computation.2 | async-start | bytes 5898240 | tf_op jit(solution)/shard_map/all_gather | solution.py:1152
  10.2 1.4 copy-start.6
  10.2 1.4 copy-start.8
  10.2 1.5 copy-start.15
  10.2 1.6 copy-start.16
  10.3 1.6 copy-start.17
  10.3 1.6 copy-start.18
  10.3 1.6 copy-start.19
  10.3 1.6 copy-start.20
  10.3 138.7 %all-gather.5.cloned.1.call-start = ((), (), s32[]{:S(2)}) async-start(), calls=%async_computation.3 | async-start | bytes 5898240 | tf_op jit(solution)/shard_map/all_gather | solution.py:1153
  11.5 378.9 %reduce-scatter.3.cloned.1.call-start = ((), (), s32[]{:S(2)}) async-start(), calls=%async_computation.4 | async-start | bytes 5898240 | tf_op jit(solution)/shard_map/reduce_scatter | solution.py:1182
  74.6 1.4 copy-start.12
  74.6 1.5 copy-start.14
  76.5 2.1 copy-start.11
  76.5 70.7 %copy-start = (s32[6,208,2]{2,1,0:T(8,128)}, s32[6,208,2]{2,1,0:T(8,128)S(1)}, u32[]{:S(2)}) copy-start(s32[6,208,2]{2,1,0:T(8,128)S(1)} %pad.45.clone) | copy-start | bytes 29956
  77.7 69.5 %copy-start.1 = (s32[6,208,2]{2,1,0:T(8,128)}, s32[6,208,2]{2,1,0:T(8,128)S(1)}, u32[]{:S(2)}) copy-start(s32[6,208,2]{2,1,0:T(8,128)S(1)} %pad.47.clone) | copy-start | bytes 29956
  198.6 194.7 %reduce-scatter.5.cloned.1.call-start = ((), (), s32[]{:S(2)}) async-start(), calls=%async_computation.5 | async-start | bytes 5898240 | tf_op jit(solution)/shard_map/reduce_scatter | solution.py:1183
  198.7 1.4 copy-start.13
  198.7 2.5 copy-start.9
  198.7 3.3 copy-start.4
  379.3 4.4 %copy-start.3 = (bf16[1248,384]{1,0:T(8,128)(2,1)S(1)}, bf16[1248,384]{1,0:T(8,128)(2,1)}, u32[]{:S(2)}) copy-start(bf16[1248,384]{1,0:T(8,128)(2,1)} %get-tuple-element.58) | copy-start | bytes 2875396
  383.8 1.6 copy-start.5
  384.1 3.2 copy-start.10
  (1 other events, 0.7 us)
Sparse Core Ops, SparseCore 0:
  10.3 41.2 all-gather.2
  53.7 36.3 all-gather.4
  198.7 56.1 reduce-scatter.2
  257.5 63.0 reduce-scatter.4

commit v2 on v1

v2 whole, which is shorter than its diff:
```python
import functools

import jax
import jax.numpy as jnp
from jax import lax
from jax.experimental import pallas as pl
from jax.experimental.pallas import tpu as pltpu
from jax.sharding import PartitionSpec as P

HEAD = 64
SEQ = 197
MESH = pl.DeviceIdType.MESH
BF = jnp.bfloat16
F32 = jnp.float32
NARROW = 4
LIMIT = 62 * 1024 * 1024
eps_norm = 1e-06


def round_up(value, step):
    return -(-value // step) * step


def norm_parts(value):
    mean_value = jnp.mean(value, axis=-1, keepdims=True)
    centred = value - mean_value
    variance = jnp.mean(centred * centred, axis=-1, keepdims=True)
    inverse = lax.rsqrt(variance + eps_norm)
    return centred * inverse, inverse


def dot_nn(a, b):
    return jnp.dot(a, b, preferred_element_type=F32)


def dot_nt(a, b):
    return lax.dot_general(a, b, (((1,), (1,)), ((), ())), preferred_element_type=F32)


def dot_tn(a, b):
    return lax.dot_general(a, b, (((0,), (0,)), ((), ())), preferred_element_type=F32)


def places():
    e, m = lax.axis_index("expert"), lax.axis_index("mp")
    c, y = lax.rem(m, 2), lax.div(m, 2)
    return e, m, c, y, m + 1 - 2 * c, lax.rem(m + 2, NARROW)


def greet(n, e, m, narrow):
    barrier = pltpu.get_barrier_semaphore()

    def wide(i, carry):
        pl.semaphore_signal(
            barrier, inc=1, device_id={"expert": lax.rem(e + i, n), "mp": m}, device_id_type=MESH
        )
        return carry

    lax.fori_loop(1, n, wide, 0)
    for other in narrow:
        pl.semaphore_signal(
            barrier, inc=1, device_id={"expert": e, "mp": other}, device_id_type=MESH
        )
    pl.semaphore_wait(barrier, n - 1 + len(narrow))


def remote(src, dst, send, recv, e, m):
    return pltpu.make_async_remote_copy(
        src_ref=src,
        dst_ref=dst,
        send_sem=send,
        recv_sem=recv,
        device_id={"expert": e, "mp": m},
        device_id_type=MESH,
    )


class Summed:
    def __init__(self, rows, part, sa, sb, tot, sems):
        self.rows, self.part, self.sa, self.sb, self.tot, self.sems = rows, part, sa, sb, tot, sems
        self.e, self.m, self.c, self.y, self.sib, self.far = places()

    def at(self, i):
        return pl.ds(pl.multiple_of(i * self.rows, 16), self.rows)

    def copy_a(self, i):
        at = self.at(i)
        return remote(
            self.part.at[1 - self.c, at],
            self.sa.at[at],
            self.sems.at[0, i],
            self.sems.at[1, i],
            self.e,
            self.sib,
        )

    def copy_b(self, i):
        at = self.at(i)
        return remote(
            self.part.at[self.c, at],
            self.sb.at[at],
            self.sems.at[2, i],
            self.sems.at[3, i],
            self.e,
            self.far,
        )

    def copy_c(self, i, half):
        at = self.at(i)
        return remote(
            self.tot.at[half, at],
            self.tot.at[half, at],
            self.sems.at[4, i],
            self.sems.at[5, i],
            self.e,
            self.sib,
        )

    def start_a(self, i):
        self.copy_a(i).start()

    def step_b(self, i):
        self.copy_a(i).wait_recv()
        at = self.at(i)
        self.part[self.c, at] = (
            self.part[self.c, at].astype(F32) + self.sa[at].astype(F32)
        ).astype(BF)
        self.copy_b(i).start()

    def step_c(self, i):
        self.copy_b(i).wait_recv()
        at = self.at(i)
        self.tot[self.c, at] = (self.part[self.c, at].astype(F32) + self.sb[at].astype(F32)).astype(
            BF
        )
        self.copy_c(i, self.c).start()

    def take(self, i):
        self.copy_c(i, 1 - self.c).wait_recv()
        at = self.at(i)
        return jnp.concatenate([self.tot[0, at].astype(F32), self.tot[1, at].astype(F32)], axis=1)

    def drain(self, images):
        def one(i, carry):
            self.copy_a(i).wait_send()
            self.copy_b(i).wait_send()
            self.copy_c(i, self.c).wait_send()
            return carry

        lax.fori_loop(0, images, one, 0)


def head_masks(width, heads, dtype, value=1.0):
    lane = lax.broadcasted_iota(jnp.int32, (1, width), 1)
    return [
        jnp.where((lane >= h * HEAD) & (lane < (h + 1) * HEAD), value, 0.0).astype(dtype)
        for h in range(heads)
    ]


def forward_kernel(
    n,
    images,
    rows,
    capq,
    direct,
    share,
    x_ref,
    g_ref,
    mat_ref,
    small_ref,
    rout_ref,
    first_ref,
    keys_ref,
    noise_ref,
    xp_ref,
    a1_ref,
    q_ref,
    k_ref,
    v_ref,
    p_ref,
    o_ref,
    h_ref,
    a2_ref,
    cols_ref,
    mats_ref,
    rpad_ref,
    vec_ref,
    b1_ref,
    xr_ref,
    gr_ref,
    gt_ref,
    raw,
    packed,
    rpad,
    ab,
    smp,
    sex,
    gb,
    oh,
    xs,
    gs,
    gts,
    wt,
    part,
    sa,
    sb,
    tot,
    ar,
    zrs,
    zls,
    zv,
    nbs,
    nbv,
    pss,
    psv,
    vss,
    vsv,
    xss,
    xsr,
    gss,
    gsr,
    tss,
    tsr,
):
    e, m, c, y, sib, far = places()
    count, width = xp_ref.shape
    half = width // 2
    lanes = keys_ref.shape[1]
    heads = p_ref.shape[0]
    quarter = heads * HEAD
    group = min(4, n)
    stride = NARROW * capq
    each = width // n
    nodes = n // 2
    node, side = lax.div(e, 2), lax.rem(e, 2)
    beside = e + 1 - 2 * side
    greet(n, e, m, [lax.rem(m + j, NARROW) for j in range(1, NARROW)])
    key0, key1 = keys_ref[0:1, :], keys_ref[1:2, :]

    def block_of(where):
        return where * 2 + side

    def right_copy(where):
        at = packed.at[block_of(where)]
        return remote(at, at, zrs.at[where], zv.at[where], jnp.minimum(e + 2, n - 1), m)

    def left_copy(where):
        at = packed.at[block_of(where)]
        return remote(at, at, zls.at[where], zv.at[where], jnp.maximum(e - 2, 0), m)

    def pair_copy(where, which):
        at = packed.at[where * 2 + which]
        return remote(at, at, nbs.at[where], nbv.at[where], beside, m)

    def small_copy(j, source):
        return remote(
            small_ref, smp.at[source], pss.at[j], psv.at[j], e, lax.rem(m + j, NARROW)
        )

    def wide_copy(i, source):
        return remote(
            sex.at[source], sex.at[source], vss.at[i], vsv.at[i], lax.rem(e + i, n), m
        )

    def forward_block(where):
        @pl.when((where <= node) & (node < nodes - 1))
        def _():
            right_copy(where).start()

        @pl.when((where >= node) & (node > 0))
        def _():
            left_copy(where).start()

        pair_copy(where, side).start()

    def forward_from(d):
        for where in (node - d, node + d):

            @pl.when((where >= 0) & (where < nodes))
            def _():
                right_copy(where).wait_recv()
                forward_block(where)

    if direct:
        packed[e] = mat_ref[...]
        forward_block(node)
        for j in range(1, NARROW):
            small_copy(j, m).start()
        smp[m] = small_ref[...]

    def pad_into(to_ref, source, cast):
        for i in range(images):
            to_ref[i * rows : i * rows + SEQ, :] = source[i * SEQ : (i + 1) * SEQ, :].astype(cast)
            to_ref[i * rows + SEQ : (i + 1) * rows, :] = jnp.zeros((rows - SEQ, width), cast)

    def build(g, src, send_buf, gates):
        for j in range(group):
            i = g * group + j
            ex = lax.rem(e + i, n)
            want = lax.broadcasted_iota(jnp.int32, (capq, lanes), 0) + (ex * stride + m * capq)
            hit0, hit1 = key0 == want, key1 == want
            oh[j * capq : (j + 1) * capq, :] = jnp.where(hit0 | hit1, 1.0, 0.0).astype(BF)
            if gates is not None:
                w = jnp.where(hit0, gates[0], 0.0) + jnp.where(hit1, gates[1], 0.0)
                ws = w[:, 0:128]
                for t in range(1, lanes // 128):
                    ws = ws + w[:, t * 128 : (t + 1) * 128]
                wt[0:capq, :] = ws
                row = jnp.sum(wt[...].T, axis=0, keepdims=True)
                gts[i] = jnp.broadcast_to(row, (8, 128))
        block = dot_nn(oh[...], src[...]).astype(BF)
        for j in range(group):
            send_buf[g * group + j] = block[j * capq : (j + 1) * capq]

    def g_copy(i, source):
        return remote(gs.at[i], gr_ref.at[source], gss.at[i], gsr.at[i], lax.rem(e + i, n), m)

    def x_copy(i, source):
        return remote(xs.at[i], xr_ref.at[source], xss.at[i], xsr.at[i], lax.rem(e + i, n), m)

    def t_copy(i, source):
        return remote(gts.at[i], gt_ref.at[source], tss.at[i], tsr.at[i], lax.rem(e + i, n), m)

    pad_into(gb, g_ref, BF)
    if lanes > count:
        gb[count:lanes, :] = jnp.zeros((lanes - count, width), BF)
        a2_ref[count:lanes, :] = jnp.zeros((lanes - count, width), BF)
    wt[...] = jnp.zeros_like(wt)

    if direct:
        for j in range(1, NARROW):
            small_copy(j, lax.rem(m + NARROW - j, NARROW)).wait_recv()
        for j in range(NARROW):
            sex[e, j] = smp[j, 0:8]
            for t in range(width // 128):
                b1_ref[j, :, t * 128 : (t + 1) * 128] = jnp.broadcast_to(
                    smp[j, 8 + t : 9 + t], (8, 128)
                )
        sex[e, NARROW] = small_ref[16:24, :]

        def start_wide(i, carry):
            wide_copy(i, e).start()
            return carry

        lax.fori_loop(1, n, start_wide, 0)

    def build_g(g, carry):
        build(g, gb, gs, None)
        return carry

    lax.fori_loop(0, n // group, build_g, 0)
    gr_ref[e] = gs[0]
    if direct:
        for d in range(1, nodes // 2):
            forward_from(d)

    raw[...] = x_ref[...].astype(F32)
    for i in range(images):
        xp_ref[i * rows : (i + 1) * rows, :] = jnp.concatenate(
            [raw[i * SEQ : (i + 1) * SEQ, :], jnp.zeros((rows - SEQ, width), F32)], axis=0
        ).astype(BF)

    if direct:
        for d in range(max(1, nodes // 2), nodes):
            forward_from(d)

        def finish_wide(i, carry):
            wide_copy(i, lax.rem(e + n - i, n)).wait_recv()
            return carry

        lax.fori_loop(1, n, finish_wide, 0)
        vec_ref[...] = jnp.zeros_like(vec_ref)
        rpad[...] = jnp.zeros_like(rpad)
        for i in range(n):
            for j in range(NARROW):
                at = (i * NARROW + j) * share
                vec_ref[:, at : at + share] = sex[i, j, :, 0:share]
            rpad[0:8, i * each : (i + 1) * each] = sex[i, NARROW, :, 0:each]
        rpad_ref[...] = rpad[...].astype(BF)
        for where in range(nodes):
            pair_copy(where, 1 - side).wait_recv()
        weights = packed[...].reshape(width, 4 * quarter)
    else:
        vec_ref[...] = small_ref[...]
        rpad_ref[...] = rout_ref[...]
        b1_ref[...] = first_ref[...]
        weights = mat_ref[...]
    for j in range(4):
        mats_ref[:, j * 256 : j * 256 + quarter] = weights[:, j * quarter : (j + 1) * quarter]
        mats_ref[:, j * 256 + quarter : (j + 1) * 256] = jnp.zeros((width, 256 - quarter), BF)
    ab[...] = jnp.zeros_like(ab)
    for mm in range(NARROW):

        @pl.when(m == mm)
        def _():
            ab[0:2, 0:quarter] = vec_ref[4:6, mm * quarter : (mm + 1) * quarter]

    def start_g(i, carry):
        g_copy(i, e).start()
        return carry

    lax.fori_loop(1, n, start_g, 0)

    summed = Summed(rows, part, sa, sb, tot, ar)
    in_q = head_masks(256, heads, BF, HEAD ** (-0.5))
    in_o = head_masks(256, heads, F32)
    key_ok = lax.broadcasted_iota(jnp.int32, (rows, rows), 1) < SEQ
    gain0, gain1 = vec_ref[0:1, :], vec_ref[1:2, :]
    shift0, shift1 = vec_ref[2:3, :], vec_ref[3:4, :]
    out_shift = vec_ref[6:7, :]

    def attend(i):
        at = summed.at(i)
        normed = (norm_parts(xp_ref[at, :].astype(F32))[0] * gain0 + shift0).astype(BF)
        a1_ref[at, :] = normed
        q = (dot_nn(normed, mats_ref[:, 0:256]) + ab[0:1, :]).astype(BF)
        k = dot_nn(normed, mats_ref[:, 256:512]).astype(BF)
        v = (dot_nn(normed, mats_ref[:, 512:768]) + ab[1:2, :]).astype(BF)
        q_ref[at, :], k_ref[at, :], v_ref[at, :] = q, k, v
        o = jnp.zeros((rows, 256), F32)
        for h in range(heads):
            s = jnp.where(key_ok, dot_nt(q * in_q[h], k), -1e30)
            top = jnp.max(s, axis=-1, keepdims=True)
            ex = jnp.exp(s - top)
            p = (ex / jnp.sum(ex, axis=-1, keepdims=True)).astype(BF)
            p_ref[h, at, :] = p
            o = o + dot_nn(p, v) * in_o[h]
        o = o.astype(BF)
        o_ref[at, :] = o
        for hh in range(2):
            part[hh, at] = dot_nt(o, mats_ref[hh * half : (hh + 1) * half, 768:1024]).astype(BF)

    def second(i):
        at = summed.at(i)
        hidden = xp_ref[at, :].astype(F32) + summed.take(i) + out_shift
        h_ref[0, at], h_ref[1, at] = hidden[:, :half], hidden[:, half:]
        a2_ref[at, :] = (norm_parts(hidden)[0] * gain1 + shift1).astype(BF)

    def tick(t, carry):
        @pl.when(t < images)
        def _():
            attend(t)
            summed.start_a(t)

        @pl.when((t >= 1) & (t <= images))
        def _():
            summed.step_b(t - 1)

        @pl.when((t >= 3) & (t <= images + 2))
        def _():
            summed.step_c(t - 3)

        @pl.when(t >= 4)
        def _():
            second(t - 4)

        return carry

    lax.fori_loop(0, images + 4, tick, 0)

    tops = noise_ref.shape[0]
    logits = dot_nt(rpad_ref[0:tops, :], a2_ref[...]) + noise_ref[...]
    floor = lax.broadcasted_iota(jnp.int32, logits.shape, 0) * stride
    picked = [
        jnp.sum(
            jnp.where((key >= floor) & (key < floor + stride), logits, 0.0), axis=0, keepdims=True
        )
        for key in (key0, key1)
    ]
    top = jnp.maximum(picked[0], picked[1])
    ex0, ex1 = jnp.exp(picked[0] - top), jnp.exp(picked[1] - top)
    gate0, gate1 = ex0 / (ex0 + ex1), ex1 / (ex0 + ex1)

    def build_x(g, carry):
        build(g, a2_ref, xs, (gate0, gate1))
        for j in range(group):
            i = g * group + j

            @pl.when(i == 0)
            def _():
                xr_ref[e] = xs[0]
                gt_ref[e] = gts[0]

            @pl.when(i > 0)
            def _():
                x_copy(i, e).start()
                t_copy(i, e).start()

        return carry

    lax.fori_loop(0, n // group, build_x, 0)
    cols_ref[...] = jnp.concatenate(
        [key0.astype(F32), key1.astype(F32), gate0, gate1, jnp.zeros((124, lanes), F32)], axis=0
    ).T

    def finish(i, carry):
        source = lax.rem(e + n - i, n)
        for copy in (g_copy, x_copy, t_copy):
            copy(i, source).wait_recv()
            copy(i, source).wait_send()
        if direct:
            wide_copy(i, e).wait_send()
        return carry

    lax.fori_loop(1, n, finish, 0)
    summed.drain(images)
    if direct:
        for j in range(1, NARROW):
            small_copy(j, m).wait_send()
        for where in range(nodes):
            pair_copy(where, side).wait_send()

            @pl.when((where <= node) & (node < nodes - 1))
            def _():
                right_copy(where).wait_send()

            @pl.when((where >= node) & (node > 0))
            def _():
                left_copy(where).wait_send()


def forward(n, images, rows, capq, heads, direct, share, x, g, mat, small, rout, first, keys, noise):
    width = x.shape[1]
    count, lanes = images * rows, keys.shape[1]
    half = width // 2
    group = min(4, n)
    sem = pltpu.SemaphoreType.DMA
    struct = jax.ShapeDtypeStruct
    outs = (
        struct((count, width), BF),
        struct((count, width), BF),
        struct((count, 256), BF),
        struct((count, 256), BF),
        struct((count, 256), BF),
        struct((heads, count, rows), BF),
        struct((count, 256), BF),
        struct((2, count, half), F32),
        struct((lanes, width), BF),
        struct((lanes, 128), F32),
        struct((width, 1024), BF),
        struct((128, width), BF),
        struct((8, width), F32),
        struct((NARROW, 8, width), F32),
        struct((n, capq, width), BF),
        struct((n, capq, width), BF),
        struct((n, 8, 128), F32),
    )
    args = (x, g, mat, small, rout, first, keys, noise)
    return pl.pallas_call(
        functools.partial(forward_kernel, n, images, rows, capq, direct, share),
        name="forward",
        out_shape=outs,
        in_specs=[pl.BlockSpec(memory_space=pltpu.VMEM)] * len(args),
        out_specs=(pl.BlockSpec(memory_space=pltpu.VMEM),) * len(outs),
        scratch_shapes=[
            pltpu.VMEM(x.shape, F32),
            pltpu.VMEM((n, *mat.shape) if direct else (1, 16, 128), BF),
            pltpu.VMEM((128, width), F32),
            pltpu.VMEM((8, 256), F32),
            pltpu.VMEM((NARROW, 24, 128), F32),
            pltpu.VMEM((n, NARROW + 1, 8, 128), F32),
            pltpu.VMEM((lanes, width), BF),
            pltpu.VMEM((group * capq, lanes), BF),
            pltpu.VMEM((n, capq, width), BF),
            pltpu.VMEM((n, capq, width), BF),
            pltpu.VMEM((n, 8, 128), F32),
            pltpu.VMEM((128, 128), F32),
            pltpu.VMEM((2, count, half), BF),
            pltpu.VMEM((count, half), BF),
            pltpu.VMEM((count, half), BF),
            pltpu.VMEM((2, count, half), BF),
            sem((6, images)),
        ]
        + [sem((n // 2,))] * 5
        + [sem((NARROW,))] * 2
        + [sem((n,))] * 8,
        compiler_params=pltpu.CompilerParams(
            collective_id=1, has_side_effects=True, vmem_limit_bytes=LIMIT
        ),
    )(*args)


def expert_kernel(
    n,
    capq,
    lanes_each,
    chunk,
    x_ref,
    g_ref,
    gt_ref,
    w1_ref,
    w2_ref,
    b1_ref,
    b2_ref,
    dxr_ref,
    dgr_ref,
    gy_ref,
    d1_ref,
    d2_ref,
    db_ref,
    gcol,
    dy,
    xt,
    yacc,
    dxacc,
    dxs,
    dgs,
    wt,
    s1,
    s2,
    r1,
    r2,
    ws,
    wv,
    dxss,
    dxsv,
    dgss,
    dgsv,
):
    e, m, c, y, sib, far = places()
    slots, width = x_ref.shape
    hidden = w1_ref.shape[2]
    greet(n, e, m, [sib, far])

    def gate_col(i, carry):
        row = jnp.broadcast_to(gt_ref[i, 0:1, :], (128, 128))
        gcol[pl.ds(pl.multiple_of(i * capq, 16), capq), :] = row.T[0:capq]
        return carry

    lax.fori_loop(0, n, gate_col, 0)
    gate = gcol[:, 0:1]
    grad = (g_ref[...].astype(F32) * gate).astype(BF)
    dy[...] = grad
    db_ref[NARROW] = jnp.broadcast_to(jnp.sum(grad.astype(F32), axis=0, keepdims=True), (8, width))
    xt[...] = x_ref[...].T
    yacc[...] = jnp.zeros_like(yacc)
    dxacc[...] = jnp.zeros_like(dxacc)
    if lanes_each > capq:
        dxr_ref[:, capq:lanes_each, :] = jnp.zeros((n, lanes_each - capq, width), BF)

    def w_copies(t, to):
        return [
            remote(s1.at[t], r1.at[t], ws.at[0, t], wv.at[0, t], e, to),
            remote(s2.at[t], r2.at[t], ws.at[1, t], wv.at[1, t], e, to),
        ]

    route = [(3 - m, sib), (far, far), (sib, sib), (m, None)]
    for t, (q, to) in enumerate(route):

        def step(j, carry):
            at = pl.ds(pl.multiple_of(j * chunk, chunk), chunk)
            w1, w2 = w1_ref[q, :, at], w2_ref[q, at, :]
            z = dot_nn(x_ref[...], w1) + b1_ref[q, 0:1, at]
            cdf = 0.5 * (1.0 + lax.erf(z * (2.0**-0.5)))
            pdf = jnp.exp(-0.5 * z * z) * ((2.0 * jnp.pi) ** -0.5)
            u = (z * cdf).astype(BF)
            yacc[...] += dot_nn(u, w2)
            dz = dot_nt(dy[...], w2) * (cdf + z * pdf)
            db_ref[q, :, at] = jnp.broadcast_to(jnp.sum(dz, axis=0, keepdims=True), (8, chunk))
            dz = dz.astype(BF)
            dxacc[...] += dot_nt(dz, w1)
            dw2 = dot_tn(u, dy[...])
            dw1 = dot_nn(xt[...], dz)
            if to is None:
                d2_ref[at, :] = dw2
                d1_ref[:, at] = dw1
            else:
                s2[t, at, :] = dw2.astype(BF)
                s1[t, :, at] = dw1.astype(BF)
            return carry

        lax.fori_loop(0, hidden // chunk, step, 0)
        if t == 1:
            for copy in w_copies(0, sib):
                copy.wait_recv()
            s1[1] = (s1[1].astype(F32) + r1[0].astype(F32)).astype(BF)
            s2[1] = (s2[1].astype(F32) + r2[0].astype(F32)).astype(BF)
        if to is not None:
            for copy in w_copies(t, to):
                copy.start()

    def dx_copy(i, to, source):
        return remote(
            dxs.at[to], dxr_ref.at[source, pl.ds(0, capq)], dxss.at[i], dxsv.at[i], to, m
        )

    def dg_copy(i, to, source):
        return remote(dgs.at[to], dgr_ref.at[source], dgss.at[i], dgsv.at[i], to, m)

    def start_dx(i, carry):
        to = lax.rem(e + i, n)
        at = pl.ds(pl.multiple_of(to * capq, 16), capq)
        dxs[to] = dxacc[at, :].astype(BF)
        dx_copy(i, to, e).start()
        return carry

    lax.fori_loop(1, n, start_dx, 0)
    own = pl.ds(pl.multiple_of(e * capq, 16), capq)
    dxr_ref[e, 0:capq, :] = dxacc[own, :].astype(BF)
    yv = yacc[...] + b2_ref[0:1, :]
    gy_ref[...] = (yv * gate).astype(BF)
    gcol[...] = jnp.broadcast_to(
        jnp.sum(yv * g_ref[...].astype(F32), axis=1, keepdims=True), gcol.shape
    )
    wt[...] = jnp.zeros_like(wt)
    dgs[...] = jnp.zeros_like(dgs)
    per = max(1, 128 // lanes_each)

    def gate_row(i, carry):
        wt[0:capq, :] = gcol[pl.ds(pl.multiple_of(i * capq, 16), capq), :]
        row = wt[...].T[0:8, :]
        for k in range(per):

            @pl.when(lax.rem(e, per) == k)
            def _():
                dgs[i, :, k * lanes_each : (k + 1) * lanes_each] = row[:, 0:lanes_each]

        return carry

    lax.fori_loop(0, n, gate_row, 0)

    def start_dg(i, carry):
        dg_copy(i, lax.rem(e + i, n), e).start()
        return carry

    lax.fori_loop(1, n, start_dg, 0)
    dgr_ref[e] = dgs[e]

    for copy in w_copies(2, sib):
        copy.wait_recv()
    d1_ref[...] += r1[2].astype(F32)
    d2_ref[...] += r2[2].astype(F32)
    for copy in w_copies(1, far):
        copy.wait_recv()
    d1_ref[...] += r1[1].astype(F32)
    d2_ref[...] += r2[1].astype(F32)

    def finish(i, carry):
        source = lax.rem(e + n - i, n)
        dx_copy(i, source, source).wait_recv()
        dg_copy(i, source, source).wait_recv()
        dx_copy(i, lax.rem(e + i, n), e).wait_send()
        dg_copy(i, lax.rem(e + i, n), e).wait_send()
        return carry

    lax.fori_loop(1, n, finish, 0)
    for t, to in ((0, sib), (1, far), (2, sib)):
        for copy in w_copies(t, to):
            copy.wait_send()


def experts(n, capq, lanes_each, x, g, gt, w1, w2, b1, b2, chunk):
    slots, width = x.shape
    hidden = w1.shape[2]
    struct = jax.ShapeDtypeStruct
    sem = pltpu.SemaphoreType.DMA
    outs = (
        struct((n, lanes_each, width), BF),
        struct((n, 8, 128), F32),
        struct((slots, width), BF),
        struct(w1.shape[1:], F32),
        struct(w2.shape[1:], F32),
        struct((NARROW + 1, 8, width), F32),
    )
    args = (x, g, gt, w1, w2, b1, b2)
    return pl.pallas_call(
        functools.partial(expert_kernel, n, capq, lanes_each, chunk),
        name="experts",
        out_shape=outs,
        in_specs=[pl.BlockSpec(memory_space=pltpu.VMEM)] * len(args),
        out_specs=(pl.BlockSpec(memory_space=pltpu.VMEM),) * len(outs),
        scratch_shapes=[
            pltpu.VMEM((slots, 128), F32),
            pltpu.VMEM((slots, width), BF),
            pltpu.VMEM((width, slots), BF),
            pltpu.VMEM((slots, width), F32),
            pltpu.VMEM((slots, width), F32),
            pltpu.VMEM((n, capq, width), BF),
            pltpu.VMEM((n, 8, 128), F32),
            pltpu.VMEM((128, 128), F32),
            pltpu.VMEM((3, width, hidden), BF),
            pltpu.VMEM((3, hidden, width), BF),
            pltpu.VMEM((3, width, hidden), BF),
            pltpu.VMEM((3, hidden, width), BF),
            sem((2, 3)),
            sem((2, 3)),
        ]
        + [sem((n,))] * 4,
        compiler_params=pltpu.CompilerParams(
            collective_id=3, has_side_effects=True, vmem_limit_bytes=LIMIT
        ),
    )(*args)


def backward_kernel(
    n,
    images,
    rows,
    capq,
    lanes_each,
    direct,
    share,
    owners,
    dxr_ref,
    dgr_ref,
    gy_ref,
    x_ref,
    g_ref,
    h_ref,
    a1_ref,
    q_ref,
    k_ref,
    v_ref,
    p_ref,
    o_ref,
    a2_ref,
    cols_ref,
    mats_ref,
    rpad_ref,
    vec_ref,
    db_ref,
    fg_ref,
    po_ref,
    pg_ref,
    small_ref,
    router_ref,
    dbo_ref,
    gyr,
    oht,
    dlog,
    part,
    sa,
    sb,
    tot,
    dh,
    part2,
    tot2,
    sa2,
    sb2,
    dq,
    dk,
    dv,
    dr,
    acc,
    mine,
    mpv,
    exv,
    pgs,
    pgr,
    ar,
    ar2,
    pss,
    gys,
    gyv,
    pgss,
    pgsr,
    mss,
    msr,
    ess,
    esr,
):
    e, m, c, y, sib, far = places()
    count, width = x_ref.shape
    half = width // 2
    heads = p_ref.shape[0]
    quarter = heads * HEAD
    each = width // n
    stride = NARROW * capq
    slots = n * lanes_each
    per = max(1, 128 // lanes_each)
    wide = acc.shape[0]
    here = pl.ds(0, capq)
    if lanes_each > capq:
        gyr[:, capq:lanes_each, :] = jnp.zeros((n, lanes_each - capq, width), BF)
    greet(n, e, m, [lax.rem(m + j, NARROW) for j in range(1, NARROW)])

    def gy_copy(i, to, source):
        return remote(gy_ref.at[to], gyr.at[source, here], gys.at[i], gyv.at[i], to, m)

    def start_gy(i, carry):
        gy_copy(i, lax.rem(e + i, n), e).start()
        return carry

    lax.fori_loop(1, n, start_gy, 0)
    gyr[e, 0:capq, :] = gy_ref[e]

    gain0, gain1 = vec_ref[0:1, :], vec_ref[1:2, :]

    lane = lax.broadcasted_iota(jnp.int32, (1, slots), 1)
    place = lane % lanes_each
    want = (lane // lanes_each) * stride + place + m * capq
    want = jnp.where(place < capq, want, -2).astype(F32)
    pieces = []
    for block in range(n // per):
        piece = dgr_ref[block * per]
        for j in range(1, per):
            piece = piece + dgr_ref[block * per + j]
        pieces.append(piece[0:1, :])
    dgrow = jnp.concatenate(pieces, axis=1)
    acc[...] = jnp.zeros_like(acc)
    dh[...] = jnp.zeros_like(dh)
    for i in range(images):
        dh[i * rows : i * rows + SEQ, :] = g_ref[i * SEQ : (i + 1) * SEQ, :]

    summed = Summed(rows, part, sa, sb, tot, ar)
    again = Summed(rows, part2, sa2, sb2, tot2, ar2)
    rfloor = lax.broadcasted_iota(jnp.int32, (1, 128), 1).astype(F32) * stride

    def returned(i):
        at = summed.at(i)
        key = [cols_ref[at, 0:1], cols_ref[at, 1:2]]
        gate = [cols_ref[at, 2:3], cols_ref[at, 3:4]]
        hits = [key[0] == want, key[1] == want]
        oht[at, :] = jnp.where(hits[0] | hits[1], 1.0, 0.0).astype(BF)
        dgate = [jnp.sum(jnp.where(hit, dgrow, 0.0), axis=1, keepdims=True) for hit in hits]
        mean = gate[0] * dgate[0] + gate[1] * dgate[1]
        dl = [
            jnp.where(
                (key[kk] >= rfloor) & (key[kk] < rfloor + stride), gate[kk] * (dgate[kk] - mean), 0.0
            )
            for kk in range(2)
        ]
        dl = (dl[0] + dl[1]).astype(BF)
        dlog[at, :] = dl
        for hh in range(2):
            cut = slice(hh * half, (hh + 1) * half)
            rowsum = dot_nn(oht[at, :], dxr_ref[:, :, cut].reshape(slots, half))
            part[hh, at] = (rowsum + dot_nn(dl, rpad_ref[:, cut])).astype(BF)

    in_b = head_masks(256, heads, BF)
    in_f = head_masks(256, heads, F32)
    scale = HEAD ** (-0.5)

    def attend(i):
        at = summed.at(i)
        da2 = summed.take(i)
        hidden = jnp.concatenate([h_ref[0, at], h_ref[1, at]], axis=1)
        normed, inverse = norm_parts(hidden)
        mixed = da2 * normed
        acc[1:2, :] += jnp.sum(mixed, axis=0, keepdims=True)
        acc[3:4, :] += jnp.sum(da2, axis=0, keepdims=True)
        mean_mixed = jnp.mean(mixed * gain1, axis=-1, keepdims=True)
        g2 = da2 * gain1
        mean_grad = jnp.mean(g2, axis=-1, keepdims=True)
        grad = dh[at, :] + inverse * (g2 - mean_grad - normed * mean_mixed)
        dh[at, :] = grad
        acc[6:7, :] += jnp.sum(grad, axis=0, keepdims=True)
        low = grad.astype(BF)
        dr[at, :] = low
        do = dot_nn(low, mats_ref[:, 768:1024]).astype(BF)
        q, k, v = q_ref[at, :], k_ref[at, :], v_ref[at, :]
        zero = jnp.zeros((rows, 256), F32)
        dqa, dka, dva = zero, zero, zero
        for h in range(heads):
            p = p_ref[h, at, :]
            dp = dot_nt(do * in_b[h], v)
            pf = p.astype(F32)
            t = pf * dp
            ds = (t - pf * jnp.sum(t, axis=-1, keepdims=True)).astype(BF)
            dqa = dqa + dot_nn(ds, k) * in_f[h]
            dka = dka + dot_tn(ds, q) * in_f[h]
            dva = dva + dot_tn(p, do) * in_f[h]
        dqb, dkb, dvb = (dqa * scale).astype(BF), (dka * scale).astype(BF), dva.astype(BF)
        dq[at, :], dk[at, :], dv[at, :] = dqb, dkb, dvb
        acc[4:5, 0:256] += jnp.sum(dqb.astype(F32), axis=0, keepdims=True)
        acc[5:6, 0:256] += jnp.sum(dvb.astype(F32), axis=0, keepdims=True)
        for hh in range(2):
            r = slice(hh * half, (hh + 1) * half)
            part2[hh, at] = (
                dot_nt(dqb, mats_ref[r, 0:256])
                + dot_nt(dkb, mats_ref[r, 256:512])
                + dot_nt(dvb, mats_ref[r, 512:768])
            ).astype(BF)

    def last(i):
        at = again.at(i)
        da1 = again.take(i)
        normed, inverse = norm_parts(x_ref[at, :].astype(F32))
        mixed = da1 * normed
        acc[0:1, :] += jnp.sum(mixed, axis=0, keepdims=True)
        acc[2:3, :] += jnp.sum(da1, axis=0, keepdims=True)
        mean_mixed = jnp.mean(mixed * gain0, axis=-1, keepdims=True)
        g1 = da1 * gain0
        mean_grad = jnp.mean(g1, axis=-1, keepdims=True)
        dh[at, :] += inverse * (g1 - mean_grad - normed * mean_mixed)

    def tick(t, carry):
        @pl.when(t < images)
        def _():
            returned(t)
            summed.start_a(t)

        @pl.when((t >= 1) & (t <= images))
        def _():
            summed.step_b(t - 1)

        @pl.when((t >= 3) & (t <= images + 2))
        def _():
            summed.step_c(t - 3)

        @pl.when((t >= 4) & (t <= images + 3))
        def _():
            attend(t - 4)
            again.start_a(t - 4)

        @pl.when((t >= 5) & (t <= images + 4))
        def _():
            again.step_b(t - 5)

        @pl.when((t >= 7) & (t <= images + 6))
        def _():
            again.step_c(t - 7)

        @pl.when(t >= 8)
        def _():
            last(t - 8)

        return carry

    lax.fori_loop(0, images + 5, tick, 0)

    def pg_copy(b, i, to, source):
        return remote(
            pgs.at[b, to], pgr.at[b, source], pgss.at[b, i], pgsr.at[b, i], to, m
        )

    pairs = [(dr, o_ref), (a1_ref, dq), (a1_ref, dk), (a1_ref, dv)]
    for b in range(2):
        for s in range(2):
            left, right = pairs[2 * b + s]
            grad = dot_tn(left[...], right[...])[:, :quarter]
            if direct:
                grad = grad.astype(BF)
                for i in range(n):
                    pgs[b, i, :, s * quarter : (s + 1) * quarter] = grad[i * each : (i + 1) * each]
            else:
                slot = 2 * b + s
                pg_ref[:, slot * quarter : (slot + 1) * quarter] = grad
        if direct:

            def start_pg(i, carry):
                pg_copy(b, i, lax.rem(e + i, n), e).start()
                return carry

            lax.fori_loop(1, n, start_pg, 0)
            pgr[b, e] = pgs[b, e]

    lax.fori_loop(images + 5, images + 8, tick, 0)
    summed.drain(images)
    again.drain(images)
    for i in range(images):
        fg_ref[i * SEQ : (i + 1) * SEQ, :] = dh[i * rows : i * rows + SEQ, :]

    acc[8:wide, :] = dot_tn(dlog[...], a2_ref[0:count, :])[0 : wide - 8]
    lane_w = lax.broadcasted_iota(jnp.int32, (1, width), 1)
    own_cols = (lane_w >= m * quarter) & (lane_w < (m + 1) * quarter)
    mine[0:8, :] = jnp.where(own_cols, acc[0:8, :], 0.0)
    mine[8:wide, :] = acc[8:wide, :]
    bias = acc[4:6, 0:quarter]
    mine[4:6, :] = jnp.zeros((2, width), F32)
    for mm in range(NARROW):

        @pl.when(m == mm)
        def _():
            mine[4:6, mm * quarter : (mm + 1) * quarter] = bias

    for j in range(NARROW + 1):
        mine[wide + j : wide + j + 1, :] = db_ref[j, 0:1, :]
    mine[wide + NARROW + 1 :, :] = jnp.zeros((8 - NARROW - 1, width), F32)

    def narrow(j, source):
        return remote(mine, mpv.at[source], mss.at[j], msr.at[j], e, lax.rem(m + j, NARROW))

    for j in range(1, NARROW):
        narrow(j, m).start()
    mpv[m] = mine[...]

    def arrive_gy(i, carry):
        source = lax.rem(e + n - i, n)
        gy_copy(i, source, source).wait_recv()
        return carry

    lax.fori_loop(1, n, arrive_gy, 0)

    def combine(i, carry):
        at = summed.at(i)
        for hh in range(2):
            cut = slice(hh * half, (hh + 1) * half)
            part[hh, at] = dot_nn(oht[at, :], gyr[:, :, cut].reshape(slots, half)).astype(BF)
        return carry

    lax.fori_loop(0, images, combine, 0)
    both = count // 2
    own = pl.ds(pl.multiple_of(c * both, 16), both)
    other = pl.ds(pl.multiple_of((1 - c) * both, 16), both)
    low_half = pl.ds(0, both)
    copy_pa = [
        remote(
            part.at[hh, other], sa.at[pl.ds(hh * both, both)], pss.at[hh], pss.at[2 + hh], e, sib
        )
        for hh in range(2)
    ]
    for copy in copy_pa:
        copy.start()

    for j in range(1, NARROW):
        narrow(j, lax.rem(m + NARROW - j, NARROW)).wait_recv()
    sums = mpv[0] + mpv[1] + mpv[2] + mpv[3]
    for mm in range(NARROW):

        @pl.when(m == mm)
        def _():
            dbo_ref[0:1, :] = sums[wide + mm : wide + mm + 1]

    dbo_ref[1:2, :] = sums[wide + NARROW : wide + NARROW + 1]
    acc[...] = sums[0:wide]
    top = pl.ds(0, exv.shape[1])

    def ex_copy(i, to, source):
        return remote(acc.at[top], exv.at[source], ess.at[i], esr.at[i], to, m)

    def start_ex(i, carry):
        ex_copy(i, lax.rem(e + i, n), e).start()
        return carry

    lax.fori_loop(1, n, start_ex, 0)
    exv[e] = acc[top, :]

    for copy in copy_pa:
        copy.wait_recv()
    for hh in range(2):
        sb2[hh * both : (hh + 1) * both] = (
            part[hh, own].astype(F32) + sa[hh * both : (hh + 1) * both].astype(F32)
        ).astype(BF)
    send_to = pl.ds(pl.multiple_of((1 - y) * both, 16), both)
    keep_at = pl.ds(pl.multiple_of(y * both, 16), both)
    copy_pb = remote(sb2.at[send_to], sa2.at[low_half], pss.at[4], pss.at[5], e, far)
    copy_pb.start()

    def finish_ex(i, carry):
        source = lax.rem(e + n - i, n)
        ex_copy(i, source, source).wait_recv()
        return carry

    lax.fori_loop(1, n, finish_ex, 0)
    total = exv[0]
    for i in range(1, n):
        total = total + exv[i]
    pick = lax.broadcasted_iota(jnp.int32, (width, 128), 0) - lax.broadcasted_iota(
        jnp.int32, (width, 128), 1
    )

    def picked(values, offset):
        return jnp.dot(
            values,
            jnp.where(pick == offset, 1.0, 0.0),
            precision=lax.Precision.HIGHEST,
            preferred_element_type=F32,
        )

    small_ref[...] = picked(total[0:8], (e * NARROW + m) * share)[:, 0:share]
    if direct:
        mixed = picked(total[8:wide], e * each)
        router_ref[...] = jnp.concatenate(
            [mixed, jnp.zeros((128 - mixed.shape[0], 128), F32)], axis=0
        ).T[0:each, 0:owners]
    else:
        router_ref[...] = acc[8:wide, :]

    copy_pb.wait_recv()
    total = sb2[keep_at].astype(F32) + sa2[low_half].astype(F32) + h_ref[y, own]
    po_ref[own, :] = total.astype(BF)
    copy_pc = remote(po_ref.at[own], po_ref.at[own], pss.at[6], pss.at[7], e, sib)
    copy_pc.start()
    wait_pc = remote(po_ref.at[other], po_ref.at[other], pss.at[6], pss.at[7], e, sib)

    if direct:
        for b in range(2):

            def finish_pg(i, carry):
                source = lax.rem(e + n - i, n)
                pg_copy(b, i, source, source).wait_recv()
                return carry

            lax.fori_loop(1, n, finish_pg, 0)
            total = pgr[b, 0].astype(F32)
            for i in range(1, n):
                total = total + pgr[b, i].astype(F32)
            pg_ref[:, b * 2 * quarter : (b + 1) * 2 * quarter] = total
    wait_pc.wait_recv()

    def drain(i, carry):
        to = lax.rem(e + i, n)
        gy_copy(i, to, e).wait_send()
        ex_copy(i, to, e).wait_send()
        if direct:
            pg_copy(0, i, to, e).wait_send()
            pg_copy(1, i, to, e).wait_send()
        return carry

    lax.fori_loop(1, n, drain, 0)
    for copy in copy_pa + [copy_pb, copy_pc] + [narrow(j, m) for j in range(1, NARROW)]:
        copy.wait_send()


def backward(n, images, rows, capq, lanes_each, direct, share, owners, *args):
    g, x, p = args[4], args[3], args[10]
    count, width = x.shape
    half = width // 2
    heads = p.shape[0]
    quarter = heads * HEAD
    slots = n * lanes_each
    each = width // n
    sem = pltpu.SemaphoreType.DMA
    struct = jax.ShapeDtypeStruct
    extra = round_up(owners, 8)
    wide = 8 + extra
    outs = (
        struct(g.shape, F32),
        struct((count, half), BF),
        struct((each if direct else width, 4 * quarter), F32),
        struct((8, share), F32),
        struct((each, owners) if direct else (extra, width), F32),
        struct((2, width), F32),
    )
    block = (2, n, each, 2 * quarter) if direct else (1, 1, 16, 128)
    return pl.pallas_call(
        functools.partial(
            backward_kernel, n, images, rows, capq, lanes_each, direct, share, owners
        ),
        name="backward",
        out_shape=outs,
        in_specs=[pl.BlockSpec(memory_space=pltpu.VMEM)] * len(args),
        out_specs=(pl.BlockSpec(memory_space=pltpu.VMEM),) * len(outs),
        scratch_shapes=[
            pltpu.VMEM((n, lanes_each, width), BF),
            pltpu.VMEM((count, slots), BF),
            pltpu.VMEM((count, 128), BF),
            pltpu.VMEM((2, count, half), BF),
            pltpu.VMEM((count, half), BF),
            pltpu.VMEM((count, half), BF),
            pltpu.VMEM((2, count, half), BF),
            pltpu.VMEM((count, width), F32),
            pltpu.VMEM((2, count, half), BF),
            pltpu.VMEM((2, count, half), BF),
            pltpu.VMEM((count, half), BF),
            pltpu.VMEM((count, half), BF),
            pltpu.VMEM((count, 256), BF),
            pltpu.VMEM((count, 256), BF),
            pltpu.VMEM((count, 256), BF),
            pltpu.VMEM((count, width), BF),
            pltpu.VMEM((wide, width), F32),
            pltpu.VMEM((wide + 8, width), F32),
            pltpu.VMEM((NARROW, wide + 8, width), F32),
            pltpu.VMEM((n, wide if direct else 8, width), F32),
            pltpu.VMEM(block, BF),
            pltpu.VMEM(block, BF),
            sem((6, images)),
            sem((6, images)),
            sem((8,)),
        ]
        + [sem((n,))] * 2
        + [sem((2, n))] * 2
        + [sem((NARROW,))] * 2
        + [sem((n,))] * 2,
        compiler_params=pltpu.CompilerParams(
            collective_id=2, has_side_effects=True, vmem_limit_bytes=LIMIT
        ),
    )(*args)


def on_device(
    features,
    norm_gains,
    norm_shifts,
    attention_bias,
    output_bias,
    project_weight,
    merge_weight,
    router_weight,
    router_noise,
    routes,
    slot_numbers,
    expand_weight,
    expand_bias,
    contract_weight,
    contract_bias,
    cotangent,
):
    count, width = features.shape
    n = lax.axis_size("expert")
    e, m = lax.axis_index("expert"), lax.axis_index("mp")
    capacity = 3 * count // n
    quarter = project_weight.shape[2]
    heads = quarter // HEAD
    images = count // SEQ
    rows = round_up(SEQ, 16)
    padded = images * rows
    lanes = round_up(padded, 128)
    capq = round_up(-(-capacity // NARROW), 16)
    lanes_each = 16
    while lanes_each < capq:
        lanes_each *= 2
    each = width // n
    direct = each % 16 == 0
    owners = router_weight.shape[1]
    extra = round_up(owners, 8)

    low = project_weight.astype(BF)
    mat = jnp.concatenate([low[:, 0], low[:, 1], low[:, 2], merge_weight.T.astype(BF)], axis=1)
    share = norm_gains.shape[1]
    packed = jnp.concatenate(
        [norm_gains, norm_shifts, attention_bias, output_bias[None], jnp.zeros((1, share), F32)]
    )
    router_low = router_weight.astype(BF)
    if direct:
        small = jnp.concatenate(
            [
                jnp.pad(packed, ((0, 0), (0, 128 - share))),
                jnp.pad(
                    expand_bias.reshape(-1, 128), ((0, 8 - expand_bias.shape[1] // 128), (0, 0))
                ),
                jnp.pad(
                    router_low.T.astype(F32), ((0, 8 - owners), (0, 128 - each))
                ),
            ]
        )
        rout = jnp.zeros((8, 128), BF)
        first = jnp.zeros((NARROW, 8, 128), F32)
    else:
        mat = lax.all_gather(mat, "expert", axis=0, tiled=True)
        small = lax.all_gather(packed, ("expert", "mp"), axis=1, tiled=True)
        rout = lax.all_gather(router_low, "expert", axis=0, tiled=True).T
        rout = jnp.pad(rout, ((0, 128 - owners), (0, 0)))
        first = lax.all_gather(expand_bias, "mp", axis=0)
        first = jnp.broadcast_to(first, (NARROW, 8, width))

    def along_lanes(value, top, fill):
        value = value.T.reshape(-1, images, SEQ)
        value = jnp.pad(
            value,
            ((0, top - value.shape[0]), (0, 0), (0, rows - SEQ)),
            constant_values=fill,
        )
        return jnp.pad(
            value.reshape(top, padded), ((0, 0), (0, lanes - padded)), constant_values=fill
        )

    keys = along_lanes(routes * (NARROW * capq) + slot_numbers, 8, -1)
    noise = along_lanes(router_noise, extra, 0)
    w1 = lax.all_gather(expand_weight[0].astype(BF), "mp", axis=0)
    w2 = lax.all_gather(contract_weight[0].astype(BF), "mp", axis=0)
    x, a1, q, k, v, p, o, h, a2, cols, mats, rpad, vecs, b1, xr, gr, gt = forward(
        n,
        images,
        rows,
        capq,
        heads,
        direct,
        share,
        features,
        cotangent,
        mat,
        small,
        rout,
        first,
        keys,
        noise,
    )
    slots = n * capq
    dxr, dgr, gy, d1, d2, db = experts(
        n,
        capq,
        lanes_each,
        xr.reshape(slots, width),
        gr.reshape(slots, width),
        gt,
        w1,
        w2,
        b1,
        contract_bias,
        256,
    )
    fg, po, pg, small, router_share, dbo = backward(
        n,
        images,
        rows,
        capq,
        lanes_each,
        direct,
        share,
        owners,
        dxr,
        dgr,
        gy.reshape(n, capq, width),
        x,
        cotangent,
        h,
        a1,
        q,
        k,
        v,
        p,
        o,
        a2,
        cols,
        mats,
        rpad,
        vecs,
        db,
    )
    po = po.reshape(images, rows, -1)[:, :SEQ].reshape(count, -1)
    block_output = lax.dynamic_slice_in_dim(po, lax.rem(m, 2) * quarter, quarter, 1)
    if not direct:
        pg = lax.psum_scatter(pg, "expert", scatter_dimension=0, tiled=True)
        router_share = lax.psum_scatter(
            router_share[:owners].T, "expert", scatter_dimension=0, tiled=True
        )
    return (
        block_output,
        fg,
        small[0:2],
        small[2:4],
        small[4:6],
        small[6],
        pg[:, quarter:].reshape(each, 3, quarter),
        pg[:, :quarter].T,
        router_share,
        d1[None],
        dbo[0:1],
        d2[None],
        dbo[1:2],
    )


def solution(mesh):
    placed = (
        P("expert", None),
        P(None, ("expert", "mp")),
        P(None, ("expert", "mp")),
        P(None, ("expert", "mp")),
        P(("expert", "mp")),
        P("expert", None, "mp"),
        P("mp", "expert"),
        P("expert", None),
        P("expert", None),
        P("expert", None),
        P("expert", None),
        P("expert", None, "mp"),
        P("expert", "mp"),
        P("expert", "mp", None),
        P("expert", None),
        P("expert", None),
    )
    return jax.shard_map(
        on_device,
        mesh=mesh,
        in_specs=placed,
        out_specs=(
            P("expert", "mp"),
            P("expert", None),
            P(None, ("expert", "mp")),
            P(None, ("expert", "mp")),
            P(None, ("expert", "mp")),
            P(("expert", "mp")),
            P("expert", None, "mp"),
            P("mp", "expert"),
            P("expert", None),
            P("expert", None, "mp"),
            P("expert", "mp"),
            P("expert", "mp", None),
            P("expert", None),
        ),
        check_vma=False,
    )
```

time: 405 us -> 333 us (0.82)
  Pallas kernels: 336 us -> 288 us
  local copies, waits for them, and re-layouts: 40.3 us -> 21.5 us
  other arithmetic: 11.4 us -> 5.49 us
    pallas_call x1, Pallas kernels: 172 us -> 90.8 us  [backward(): pl.pallas_call(functools.partial(backward_kernel, n, images, rows, capq,...]
    pallas_call x3 -> x2, Pallas kernels: 164 us -> 197 us  [the longest x1 98.6 us: forward(): pl.pallas_call(functools.partial(forward_kernel, n, images, rows, capq, d...]
    reshape x9 -> x5, local copies, waits for them, and re-layouts: 11.3 us -> 0.6 us  [the longest x1 0.27 us: on_device(): po = po.reshape(images, rows, -1)[:, :SEQ].reshape(count, -1)]
    pad x11 -> x4, local copies, waits for them, and re-layouts: 9.02 us -> 1.27 us  [the longest x2 1.25 us: along_lanes(): jnp.pad(value.reshape(top, padded), ((0, 0), (0, lanes - padded)), consta...]
    unnamed x51 -> x40, local copies, waits for them, and re-layouts: 4.65 us -> 11.6 us
    convert_element_type x3 -> x1, other arithmetic: 5.7 us -> 0.01 us  [on_device(): router_low.T.astype(F32)]
    slice x11 -> x5, local copies, waits for them, and re-layouts: 9.62 us -> 4.43 us  [the longest x1 1.35 us: on_device(): small[4:6]]
  transfers between devices with their start and end apart: 4 -> 2, of which waited for: 0 -> 0; matrix products, arithmetic and copies ran while one was open for 11% -> 2% of each run, Pallas kernels for 71% -> 30%
where the time goes in v2:
time: 333 us; the launch traced here: 330 us
  Pallas kernels  288 us (86%)
  local copies, waits for them, and re-layouts  21.5 us (6%)
  between operations  14.6 us (4%)
  other arithmetic  5.49 us (2%)
    pallas_call x1, Pallas kernels, forward(): pl.pallas_call(functools.partial(forward_kernel, n, images, rows, capq, d...  98.6 us
    pallas_call x1, Pallas kernels, experts(): pl.pallas_call(functools.partial(expert_kernel, n, capq, lanes_each, chun...  98.5 us
    pallas_call x1, Pallas kernels, backward(): pl.pallas_call(functools.partial(backward_kernel, n, images, rows, capq,...  90.8 us
    unnamed x40, local copies, waits for them, and re-layouts  11.6 us
  transfers between devices with their start and end apart: 2, of which 0 were waited for; matrix products, arithmetic and copies ran while one was open for 2% of the time, Pallas kernels for 30%

profile of v2, /device:TPU:0, one launch (start us, length us, event | category | flops | bytes accessed | tf_op | source)
XLA Modules:
  0.0 329.6 jit_solution(10632461628278063348)
XLA Ops:
  7.2 2.9 convert_element_type.39
  10.4 1.1 convert_element_type.40
  11.9 0.6 pad.38.noise_ref
  12.7 0.6 pad.36.keys_ref
  13.5 0.6 fusion.small_ref
  14.1 0.8 pad_maximum_fusion.mat_ref
  14.9 0.6 broadcast_in_dim.17.first_ref
  16.1 98.6 %forward.1 = (bf16[1248,768]{1,0:T(8,128)(2,1)}, bf16[1248,768]{1,0:T(8,128)(2,1)}, bf16[1248,256]{1,0:T(8,128)(2,1)}, bf16[1248,256]{1,0:T(8,128)(2,1)}, bf16[1...) custom-call(bf16[1182,768]{1,0:T(8,128)(2,1)} %x_ref.1, ...), custom_call_target="tpu_custom_call" | custom-call | tf_op jit(solution)/shard_map/forward/pallas_call | solution.py:550
  114.7 98.5 %experts.1 = (bf16[8,128,768]{2,1,0:T(8,128)(2,1)}, f32[8,8,128]{2,1,0:T(8,128)}, bf16[896,768]{1,0:T(8,128)(2,1)}, f32[768,768]{1,0:T(8,128)}, f32[768,768]{1,0:T(8,128)}, /*index=5*/f32[5,8,768]{2,1,0:T(8,128)}) custom-call(bf16[896,768]{1,0:T(8,128)(2,1)} %bitcast.29, bf16[896,768]{1,0:T(8,128)(2,1)} %bitcast.30, f32[8,8,128]{2,1,0:T(8,128)} %get-tuple-element.44.gt_ref, ...), custom_call_target="tpu_custom_call" | custom-call | tf_op jit(solution)/shard_map/experts/pallas_call | solution.py:767
  213.2 90.8 %backward.1 = (f32[1182,768]{1,0:T(8,128)}, bf16[1248,384]{1,0:T(8,128)(2,1)}, f32[96,768]{1,0:T(8,128)}, f32[8,24]{1,0:T(8,128)}, f32[96,8]{1,0:T(8,128)}, /*index=5*/f32[2,768]{1,0:T(2,128)}) custom-call(bf16[8,128,768]{2,1,0:T(8,128)(2,1)} %get-tuple-element.46.dxr_ref, f32[8,8,128]{2,1,0:T(8,128)} %get-tuple-element.47.dgr_ref, ...), custom_call_target="tpu_custom_call" | custom-call | tf_op jit(solution)/shard_map/backward/pallas_call | solution.py:1228
  304.0 1.1 slice.44
  305.1 0.9 slice_bitcast_fusion
  306.0 1.4 fusion.3
  307.3 1.2 slice_bitcast_fusion.4
  308.5 1.3 slice.51
  310.4 1.0 copy.42
  311.5 0.9 copy.43
  312.4 0.7 copy.44
  313.1 0.6 fusion.2
  313.7 0.7 copy.45
  314.4 4.2 %copy.49 = f32[1182,768]{1,0:T(8,128)} copy(f32[1182,768]{1,0:T(8,128)} %get-tuple-element.132) | data formatting | bytes 7262208
  318.6 1.4 copy.50
  320.0 1.1 copy-done.1
  321.1 1.4 copy.51
  (56 shorter events, 2.0 us)
Async XLA Ops:
  7.2 3.2 copy-start
  7.2 107.4 %all-gather.3.cloned.1.call-start = ((), (), s32[]{:S(2)}) async-start(), calls=%async_computation | async-start | bytes 5898240 | tf_op jit(solution)/shard_map/all_gather | solution.py:1352
  10.2 1.4 copy-start.3
  10.2 1.4 copy-start.4
  10.2 1.5 copy-start.6
  10.2 2.3 copy-start.7
  10.3 2.3 copy-start.8
  10.3 3.1 copy-start.11
  10.3 3.1 copy-start.12
  10.3 3.1 copy-start.13
  10.3 3.1 copy-start.14
  10.3 3.1 copy-start.15
  10.3 3.1 copy-start.10
  10.3 104.3 %all-gather.5.cloned.1.call-start = ((), (), s32[]{:S(2)}) async-start(), calls=%async_computation.1 | async-start | bytes 5898240 | tf_op jit(solution)/shard_map/all_gather | solution.py:1353
  309.8 3.3 %copy-start.9 = (f32[2,768]{1,0:T(2,128)S(1)}, f32[2,768]{1,0:T(2,128)}, u32[]{:S(2)}) copy-start(f32[2,768]{1,0:T(2,128)} %get-tuple-element.69) | copy-start | bytes 18436
  309.8 3.9 %copy-start.5 = (f32[96,8]{1,0:T(8,128)S(1)}, f32[96,8]{1,0:T(8,128)}, u32[]{:S(2)}) copy-start(f32[96,8]{1,0:T(8,128)} %get-tuple-element.105) | copy-start | bytes 9220
  314.4 4.2 %copy-start.2 = (f32[768,768]{1,0:T(8,128)S(1)}, f32[768,768]{1,0:T(8,128)}, u32[]{:S(2)}) copy-start(f32[768,768]{1,0:T(8,128)} %get-tuple-element.68) | copy-start | bytes 7077892
  318.6 2.5 copy-start.1
Sparse Core Ops, SparseCore 0:
  10.3 40.6 all-gather.2
  53.2 45.9 all-gather.4
